TPU v7x, 32 devices: a whole 2x2x4 slice. The times are simulated.
32 devices in a mesh: dp: 8 (over y, x, core), mp: 4 (over z).
Axes of the slice: x: 2, y: 2, z: 4, core: 2. Of those that a mesh axis runs over, the one named last changes fastest.
Arguments:
- patches: bfloat16 [12288, 768], P(('dp', 'mp')), may hold values from -6 to 6
- cotangent: bfloat16 [12288, 768], P(('dp', 'mp')), may hold values from -6 to 6
- conditioning: bfloat16 [24, 768], P('dp'), may hold values from -6 to 6
- lengths: int32 [8, 3], P('dp'), may hold values from 1 to 768, 1536 in all within a row
- routes: int32 [12288, 2], P('dp'), may hold values from 0 to 7, all different within a row; in each aligned block of 1536 rows (0 to 1535, 1536 to 3071, ...) at most 480 rows name the same one
- ada_weight: float32 [768, 4608], P(None, ('dp', 'mp')), may hold values from -0.21875 to 0.21875
- ada_first: float32 [768, 4608], P(None, ('dp', 'mp')), may hold values from -32 to 32
- ada_second: float32 [768, 4608], P(None, ('dp', 'mp')), may hold values from 81.1008 to 1290.24
- router_weight: float32 [6144], P(('dp', 'mp')), may hold values from -0.15625 to 0.15625
- router_first: float32 [6144], P(('dp', 'mp')), may hold values from -32 to 32
- router_second: float32 [6144], P(('dp', 'mp')), may hold values from 81.1008 to 1290.24
- qkv_weight: float32 [768, 2304], P('dp', 'mp'), may hold values from -0.21875 to 0.21875
- qkv_first: float32 [768, 2304], P('dp', 'mp'), may hold values from -20 to 20
- qkv_second: float32 [768, 2304], P('dp', 'mp'), may hold values from 29.4912 to 466.944
- proj_weight: float32 [768, 768], P('mp', 'dp'), may hold values from -1.5 to 1.5
- proj_first: float32 [768, 768], P('mp', 'dp'), may hold values from -32 to 32
- proj_second: float32 [768, 768], P('mp', 'dp'), may hold values from 61.44 to 983.04
- shared_in_weight: float32 [768, 3072], P('dp', 'mp'), may hold values from -0.21875 to 0.21875
- shared_in_first: float32 [768, 3072], P('dp', 'mp'), may hold values from -28 to 28
- shared_in_second: float32 [768, 3072], P('dp', 'mp'), may hold values from 51.6096 to 823.296
- shared_out_weight: float32 [3072, 768], P('mp', 'dp'), may hold values from -0.109375 to 0.109375
- shared_out_first: float32 [3072, 768], P('mp', 'dp'), may hold values from -28 to 28
- shared_out_second: float32 [3072, 768], P('mp', 'dp'), may hold values from 51.6096 to 823.296
- expert_in_weight: float32 [8, 768, 3072], P(None, 'dp', 'mp'), may hold values from -0.21875 to 0.21875
- expert_in_first: float32 [8, 768, 3072], P(None, 'dp', 'mp'), may hold values from -7 to 7
- expert_in_second: float32 [8, 768, 3072], P(None, 'dp', 'mp'), may hold values from 3.19488 to 51.6096
- expert_out_weight: float32 [8, 3072, 768], P(None, 'mp', 'dp'), may hold values from -0.109375 to 0.109375
- expert_out_first: float32 [8, 3072, 768], P(None, 'mp', 'dp'), may hold values from -7 to 7
- expert_out_second: float32 [8, 3072, 768], P(None, 'mp', 'dp'), may hold values from 3.19488 to 51.6096
Outputs:
- result: bfloat16 [12288, 768], P(('dp', 'mp'))
- patch_grad: bfloat16 [12288, 768], P(('dp', 'mp'))
- ada_weight_new: float32 [768, 4608], P(None, ('dp', 'mp'))
- ada_first_new: float32 [768, 4608], P(None, ('dp', 'mp'))
- ada_second_new: float32 [768, 4608], P(None, ('dp', 'mp'))
- ada_weight_low: bfloat16 [768, 4608], P(None, ('dp', 'mp'))
- router_weight_new: float32 [6144], P(('dp', 'mp'))
- router_first_new: float32 [6144], P(('dp', 'mp'))
- router_second_new: float32 [6144], P(('dp', 'mp'))
- router_weight_low: bfloat16 [6144], P(('dp', 'mp'))
- qkv_weight_new: float32 [768, 2304], P('dp', 'mp')
- qkv_first_new: float32 [768, 2304], P('dp', 'mp')
- qkv_second_new: float32 [768, 2304], P('dp', 'mp')
- qkv_weight_low: bfloat16 [768, 2304], P('dp', 'mp')
- proj_weight_new: float32 [768, 768], P('mp', 'dp')
- proj_first_new: float32 [768, 768], P('mp', 'dp')
- proj_second_new: float32 [768, 768], P('mp', 'dp')
- proj_weight_low: bfloat16 [768, 768], P('mp', 'dp')
- shared_in_weight_new: float32 [768, 3072], P('dp', 'mp')
- shared_in_first_new: float32 [768, 3072], P('dp', 'mp')
- shared_in_second_new: float32 [768, 3072], P('dp', 'mp')
- shared_in_weight_low: bfloat16 [768, 3072], P('dp', 'mp')
- shared_out_weight_new: float32 [3072, 768], P('mp', 'dp')
- shared_out_first_new: float32 [3072, 768], P('mp', 'dp')
- shared_out_second_new: float32 [3072, 768], P('mp', 'dp')
- shared_out_weight_low: bfloat16 [3072, 768], P('mp', 'dp')
- expert_in_weight_new: float32 [8, 768, 3072], P(None, 'dp', 'mp')
- expert_in_first_new: float32 [8, 768, 3072], P(None, 'dp', 'mp')
- expert_in_second_new: float32 [8, 768, 3072], P(None, 'dp', 'mp')
- expert_in_weight_low: bfloat16 [8, 768, 3072], P(None, 'dp', 'mp')
- expert_out_weight_new: float32 [8, 3072, 768], P(None, 'mp', 'dp')
- expert_out_first_new: float32 [8, 3072, 768], P(None, 'mp', 'dp')
- expert_out_second_new: float32 [8, 3072, 768], P(None, 'mp', 'dp')
- expert_out_weight_low: bfloat16 [8, 3072, 768], P(None, 'mp', 'dp')
Inputs may be any that keep to these rules, and one draw needn't show every extreme that they name: Each group's 3 lengths add up to 1536; the largest is exactly 768. `routes`: A row names two different experts; within each group's 1536 rows no expert is named by more than 480 rows, a bound that some block reaches.
All inputs are finite; a program needn't handle non-finite values.
Results may differ from a plain program's by a relative error of at most 0.033.
The roundings to bfloat16 on the way count: a program that leaves them out, or rounds other values in their place, can miss the bound.
Values may be sent and summed in bfloat16 or wider, within the bound.
No kernel may reach another device: no remote copies, remote signals or barrier semaphores. Data moves between devices by JAX's collectives and lax.ppermute only.
A program may use at most 256 MiB of HBM per device.

v0:
```python
import functools
import math

import jax
import jax.numpy as jnp
import numpy as np
from jax import lax
from jax.experimental import pallas as pl
from jax.experimental.pallas import tpu as pltpu
from jax.sharding import PartitionSpec as P

H = 12
HD = 64
E = 8
STEP = 10

beta_one = 0.9
beta_two = 0.95
epsilon = 1e-08
weight_decay = 0.1
norm_floor = 1e-06
highest = lax.Precision.HIGHEST
f32 = jnp.float32
bf16 = jnp.bfloat16


def norm_parts(values):
    centred = values - jnp.mean(values, axis=1, keepdims=True)
    inverse = lax.rsqrt(jnp.mean(centred * centred, axis=1, keepdims=True) + norm_floor)
    return centred * inverse, inverse


def norm_back(normed, inverse, gradient):
    first = jnp.mean(gradient, axis=1, keepdims=True)
    second = jnp.mean(gradient * normed, axis=1, keepdims=True)
    return inverse * (gradient - first - normed * second)


def after(values, *earlier):
    return lax.optimization_barrier((values, earlier))[0]


def ring_gather(block):
    width = lax.axis_size("mp")
    return [block] + [
        lax.ppermute(block, "mp", [(i, (i + shift) % width) for i in range(width)])
        for shift in range(1, width)
    ]


def sent_beside(terms, near, far):
    width = len(terms)
    first = [i for i in range(1, width) if i in (1, width - 1)]
    later = [i for i in range(1, width) if i not in first]
    got, near = lax.optimization_barrier(([terms[i] for i in first], near))
    rest, far = lax.optimization_barrier(([terms[i] for i in later], far(near)))
    found = dict(zip(first + later, got + rest))
    return [terms[0]] + [found[i] for i in range(1, width)], near, far


def ring_scatter(partial):
    width = lax.axis_size("mp")
    extent = partial.shape[0] // width
    parts = [partial[i * extent : (i + 1) * extent] for i in range(width)]
    return parts[:1] + [
        lax.ppermute(parts[shift], "mp", [(i, (i - shift) % width) for i in range(width)])
        for shift in range(1, width)
    ]


LANES = 128
VMEM = 60 * 2**20
SMALL = pl.CostEstimate(flops=10**6, bytes_accessed=10**5, transcendentals=0)
Q_BLOCK = 256
FAR = 2.0**50
NT = (((1,), (1,)), ((), ()))
TN = (((0,), (0,)), ((), ()))
NN = (((1,), (0,)), ((), ()))


def dot(a, b, dims=NN):
    return lax.dot_general(a, b, dims, preferred_element_type=f32)


def key_widths(group):
    return sorted({min(w, group) for w in (512, 768, 1024, group)})


def key_windows(lengths, group):
    ends = jnp.cumsum(lengths)
    begins = ends - lengths
    first = jnp.arange(group // Q_BLOCK, dtype=jnp.int32) * Q_BLOCK
    last = first + Q_BLOCK - 1
    low = jnp.max(jnp.where(begins[None, :] <= first[:, None], begins[None, :], 0), axis=1)
    high = jnp.min(jnp.where(ends[None, :] > last[:, None], ends[None, :], group), axis=1)
    low = low // LANES * LANES
    widths = jnp.array(key_widths(group), jnp.int32)
    kind = jnp.sum((high - low)[:, None] > widths[None, :], axis=1).astype(jnp.int32)
    return jnp.minimum(low, group - widths[kind]).astype(jnp.int32), kind


def attend_kernel(start_ref, kind_ref, qkv_ref, mixed_ref, log_ref, *, group):
    block = pl.program_id(1)
    rows = pl.ds(pl.multiple_of(block * Q_BLOCK, Q_BLOCK), Q_BLOCK)
    query = qkv_ref[rows, 0:LANES] * jnp.asarray(HD**-0.5, bf16)
    for index, extent in enumerate(key_widths(group)):

        @pl.when(kind_ref[block] == index)
        def _():
            keys = pl.ds(pl.multiple_of(start_ref[block], LANES), extent)
            scores = dot(qkv_ref[keys, LANES : 2 * LANES], query, NT)
            peak = jnp.max(scores, axis=0, keepdims=True)
            exps = jnp.exp(scores - peak)
            total = jnp.sum(exps, axis=0, keepdims=True)
            probs = (exps * (1.0 / total)).astype(bf16)
            mixed = dot(qkv_ref[keys, 2 * LANES : 3 * LANES], probs, TN)
            mixed_ref[...] = mixed[:HD].astype(bf16)
            log_ref[...] = (peak + jnp.log(total))[None]


def attend(qkv, start, kind):
    group = qkv.shape[0]
    heads = qkv.shape[1] // (3 * LANES)
    blocks = group // Q_BLOCK
    return pl.pallas_call(
        functools.partial(attend_kernel, group=group),
        out_shape=(
            jax.ShapeDtypeStruct((heads * HD, group), bf16),
            jax.ShapeDtypeStruct((heads, 1, group), f32),
        ),
        grid_spec=pltpu.PrefetchScalarGridSpec(
            num_scalar_prefetch=2,
            grid=(heads, blocks),
            in_specs=[pl.BlockSpec((group, 3 * LANES), lambda h, i, *_: (0, h))],
            out_specs=(
                pl.BlockSpec((HD, Q_BLOCK), lambda h, i, *_: (h, i)),
                pl.BlockSpec((1, 1, Q_BLOCK), lambda h, i, *_: (h, 0, i)),
            ),
        ),
        compiler_params=pltpu.CompilerParams(vmem_limit_bytes=VMEM),
        cost_estimate=SMALL,
        name="attend",
    )(start, kind, qkv)


def attend_back_kernel(
    start_ref, kind_ref, qkv_ref, grad_ref, log_ref, out_ref, key_total, value_total, *, group
):
    block = pl.program_id(1)

    @pl.when(block == 0)
    def _():
        key_total[...] = jnp.zeros_like(key_total)
        value_total[...] = jnp.zeros_like(value_total)

    rows = pl.ds(pl.multiple_of(block * Q_BLOCK, Q_BLOCK), Q_BLOCK)
    scaling = HD**-0.5
    query = qkv_ref[rows, 0:LANES] * jnp.asarray(scaling, bf16)
    grad = grad_ref[...]
    kept = lax.broadcasted_iota(jnp.int32, (1, LANES), 1) < HD
    for index, extent in enumerate(key_widths(group)):

        @pl.when(kind_ref[block] == index)
        def _():
            keys = pl.ds(pl.multiple_of(start_ref[block], LANES), extent)
            key_rows = qkv_ref[keys, LANES : 2 * LANES]
            value_rows = qkv_ref[keys, 2 * LANES : 3 * LANES]
            probs = jnp.exp(dot(key_rows, query, NT) - log_ref[0])
            grad_probs = dot(value_rows[:, :HD], grad)
            middle = jnp.sum(probs * grad_probs, axis=0, keepdims=True)
            grad_scores = (probs * (grad_probs - middle)).astype(bf16)
            value_total[keys, :HD] += dot(probs.astype(bf16), grad, NT)
            key_total[keys, :] += dot(grad_scores, query)
            grad_query = dot(key_rows, grad_scores, TN).T * scaling
            out_ref[rows, 0:LANES] = jnp.where(kept, grad_query, 0.0).astype(bf16)

    @pl.when(block == pl.num_programs(1) - 1)
    def _():
        out_ref[:, LANES : 2 * LANES] = jnp.where(kept, key_total[...], 0.0).astype(bf16)
        out_ref[:, 2 * LANES : 3 * LANES] = value_total[...].astype(bf16)


def attend_back(qkv, grad_mixed, logs, start, kind):
    group = qkv.shape[0]
    heads = qkv.shape[1] // (3 * LANES)
    blocks = group // Q_BLOCK
    return pl.pallas_call(
        functools.partial(attend_back_kernel, group=group),
        out_shape=jax.ShapeDtypeStruct(qkv.shape, bf16),
        grid_spec=pltpu.PrefetchScalarGridSpec(
            num_scalar_prefetch=2,
            grid=(heads, blocks),
            in_specs=[
                pl.BlockSpec((group, 3 * LANES), lambda h, i, *_: (0, h)),
                pl.BlockSpec((HD, Q_BLOCK), lambda h, i, *_: (h, i)),
                pl.BlockSpec((1, 1, Q_BLOCK), lambda h, i, *_: (h, 0, i)),
            ],
            out_specs=pl.BlockSpec((group, 3 * LANES), lambda h, i, *_: (0, h)),
            scratch_shapes=[pltpu.VMEM((group, LANES), f32), pltpu.VMEM((group, LANES), f32)],
        ),
        compiler_params=pltpu.CompilerParams(vmem_limit_bytes=VMEM),
        cost_estimate=SMALL,
        name="attend_back",
    )(start, kind, qkv, grad_mixed, logs)


def item_rows(table_ref, term, width, segment, items):
    columns = slice(term * width, (term + 1) * width)
    rows = table_ref[0:1, columns]
    for item in range(1, items):
        rows = jnp.where(segment >= item, table_ref[item : item + 1, columns], rows)
    return rows


def item_sums(values, segment, items):
    return jnp.concatenate(
        [jnp.sum(jnp.where(segment == item, values, 0.0), axis=0, keepdims=True) for item in range(items)], axis=0
    )


def placed(width_mp):
    return lambda i, rank: (lax.rem(rank[0] - i + width_mp, width_mp), 0)


def plain(*shape):
    return pl.BlockSpec(shape, lambda i, rank: (0,) * len(shape))


def image_marks(heads, items):
    marks = np.zeros((items, heads, 3, LANES), np.float32)
    for image in range(items):
        for item in range(items):
            if image == item:
                marks[image, :, 0, HD + item] = FAR
            else:
                marks[image, :, 1, HD + item] = -FAR
    return marks.reshape(items, heads * 3 * LANES)


def norm_one_kernel(*refs, width_mp, items):
    rank_ref, segment_ref, table_ref, marks_ref, weight_ref = refs[:5]
    block_refs, (rows_ref, h_ref, qkv_ref, wide_ref) = refs[5:-4], refs[-4:]
    segment = segment_ref[...]
    width = rows_ref.shape[1]

    @pl.when(pl.program_id(0) == 0)
    def _():
        wide_ref[...] = jnp.zeros_like(wide_ref)
        for part in range(weight_ref.shape[1] // HD):
            wide_ref[:, part * LANES : part * LANES + HD] = weight_ref[:, part * HD : (part + 1) * HD]

    for place in range(width_mp):

        @pl.when(pl.program_id(0) == place)
        def _():
            rows_ref[...] = block_refs[place][...]

    normed, _ = norm_parts(rows_ref[...].astype(f32))
    shift = item_rows(table_ref, 0, width, segment, items)
    scale = item_rows(table_ref, 1, width, segment, items)
    h_one = (normed * (1.0 + scale) + shift).astype(bf16)
    h_ref[...] = h_one
    marks = item_rows(marks_ref, 0, qkv_ref.shape[1], segment, items)
    qkv_ref[...] = (dot(h_one, wide_ref[...]) + marks).astype(bf16)


def norm_one(arrays, rows, table, segment, weight):
    width_mp, width, items = len(arrays), arrays[0].shape[1], table.shape[0]
    heads = weight.shape[1] // (3 * HD)
    wide = heads * 3 * LANES
    marks = jnp.asarray(image_marks(heads, items))
    order = placed(width_mp)
    return pl.pallas_call(
        functools.partial(norm_one_kernel, width_mp=width_mp, items=items),
        out_shape=(
            jax.ShapeDtypeStruct((rows * width_mp, width), bf16),
            jax.ShapeDtypeStruct((rows * width_mp, width), bf16),
            jax.ShapeDtypeStruct((rows * width_mp, wide), bf16),
            jax.ShapeDtypeStruct((width, wide), bf16),
        ),
        grid_spec=pltpu.PrefetchScalarGridSpec(
            num_scalar_prefetch=1,
            grid=(width_mp,),
            in_specs=[pl.BlockSpec((rows, 1), order), plain(*table.shape), plain(*marks.shape), plain(*weight.shape)]
            + [plain(rows, width)] * len(arrays),
            out_specs=(
                pl.BlockSpec((rows, width), order),
                pl.BlockSpec((rows, width), order),
                pl.BlockSpec((rows, wide), order),
                plain(width, wide),
            ),
        ),
        compiler_params=pltpu.CompilerParams(vmem_limit_bytes=VMEM),
        cost_estimate=SMALL,
        name="norm_one",
    )(lax.axis_index("mp").reshape(1), segment, table, marks, weight, *arrays)


def gated_kernel(*refs, width_mp, items):
    rank_ref, segment_ref, table_ref = refs[:3]
    block_refs, out_ref = refs[3:-1], refs[-1]
    segment = segment_ref[...]
    width = out_ref.shape[1]
    for place in range(width_mp):

        @pl.when(pl.program_id(0) == place)
        def _():
            rows = block_refs[place][...].astype(f32)
            out_ref[...] = (item_rows(table_ref, 5, width, segment, items) * rows).astype(bf16)


def by_rows(kernel, outputs, arrays, rows, table, segment, name):
    width_mp, width, items = len(arrays), arrays[0].shape[1], table.shape[0]
    order = placed(width_mp)
    return pl.pallas_call(
        functools.partial(kernel, width_mp=width_mp, items=items),
        out_shape=(jax.ShapeDtypeStruct((rows * width_mp, width), bf16),) * outputs,
        grid_spec=pltpu.PrefetchScalarGridSpec(
            num_scalar_prefetch=1,
            grid=(width_mp,),
            in_specs=[pl.BlockSpec((rows, 1), order), plain(*table.shape)]
            + [plain(rows, width)] * len(arrays),
            out_specs=(pl.BlockSpec((rows, width), order),) * outputs,
        ),
        compiler_params=pltpu.CompilerParams(vmem_limit_bytes=VMEM),
        cost_estimate=SMALL,
        name=name,
    )(lax.axis_index("mp").reshape(1), segment, table, *arrays)


def norm_two_kernel(*refs, width_mp, items):
    rank_ref, segment_ref, table_ref, rows_ref, turned_ref = refs[:5]
    mixed_refs = refs[5:-6]
    h_ref, x_mine_ref, attn_mine_ref, mixed_mine_ref, proj_ref, proj_scratch = refs[-6:]
    step = pl.program_id(0)
    rank = rank_ref[0]
    segment = segment_ref[...]
    width = rows_ref.shape[1]
    heads = mixed_refs[0].shape[0]

    @pl.when(step == 0)
    def _():
        proj_scratch[...] = turned_ref[...].T
        proj_ref[...] = proj_scratch[...]

    attn = jnp.zeros(rows_ref.shape, f32)
    for place in range(width_mp):
        here = slice(place * heads, (place + 1) * heads)
        mixed = mixed_refs[place][...]
        attn += dot(mixed, proj_scratch[here, :], TN)

        @pl.when(step == rank)
        def _():
            mixed_mine_ref[here, :] = mixed

    x_one = rows_ref[...].astype(f32) + item_rows(table_ref, 2, width, segment, items) * attn

    @pl.when(step == rank)
    def _():
        x_mine_ref[...] = x_one
        attn_mine_ref[...] = attn

    normed, _ = norm_parts(x_one)
    shift = item_rows(table_ref, 3, width, segment, items)
    scale = item_rows(table_ref, 4, width, segment, items)
    h_ref[...] = (normed * (1.0 + scale) + shift).astype(bf16)


def norm_two(arrays, patches, proj_t, table, segment):
    width_mp, (heads, group) = len(arrays), arrays[0].shape
    rows, width, items = group // width_mp, patches.shape[1], table.shape[0]
    every = heads * width_mp
    return pl.pallas_call(
        functools.partial(norm_two_kernel, width_mp=width_mp, items=items),
        out_shape=(
            jax.ShapeDtypeStruct((group, width), bf16),
            jax.ShapeDtypeStruct((rows, width), f32),
            jax.ShapeDtypeStruct((rows, width), f32),
            jax.ShapeDtypeStruct((every, rows), bf16),
            jax.ShapeDtypeStruct((every, width), bf16),
        ),
        grid_spec=pltpu.PrefetchScalarGridSpec(
            num_scalar_prefetch=1,
            grid=(width_mp,),
            in_specs=[
                pl.BlockSpec((rows, 1), lambda i, rank: (i, 0)),
                plain(*table.shape),
                pl.BlockSpec((rows, width), lambda i, rank: (i, 0)),
                plain(*proj_t.shape),
            ]
            + [pl.BlockSpec((heads, rows), lambda i, rank: (0, i))] * len(arrays),
            out_specs=(
                pl.BlockSpec((rows, width), lambda i, rank: (i, 0)),
                plain(rows, width),
                plain(rows, width),
                plain(every, rows),
                plain(every, width),
            ),
            scratch_shapes=[pltpu.VMEM((every, width), bf16)],
        ),
        compiler_params=pltpu.CompilerParams(vmem_limit_bytes=VMEM),
        cost_estimate=SMALL,
        name="norm_two",
    )(lax.axis_index("mp").reshape(1), segment, table, patches, proj_t, *arrays)


def product_kernel(rank_ref, a_ref, b_ref, part_ref, out_ref):
    rows = a_ref.shape[0]
    out_ref[0:rows, :] = dot(a_ref[...], b_ref[...], NT).astype(bf16)
    out_ref[rows:, :] = part_ref[0]


def ring_product(a, b, parts):
    width_mp, extra, width = parts.shape
    rows = a.shape[0] // width_mp
    return pl.pallas_call(
        product_kernel,
        out_shape=jax.ShapeDtypeStruct((a.shape[0] + width_mp * extra, width), bf16),
        grid_spec=pltpu.PrefetchScalarGridSpec(
            num_scalar_prefetch=1,
            grid=(width_mp,),
            in_specs=[
                pl.BlockSpec((rows, a.shape[1]), placed(width_mp)),
                plain(*b.shape),
                pl.BlockSpec((1, extra, width), lambda i, rank: (i, 0, 0)),
            ],
            out_specs=pl.BlockSpec((rows + extra, width), lambda i, rank: (i, 0)),
        ),
        compiler_params=pltpu.CompilerParams(vmem_limit_bytes=VMEM),
        cost_estimate=SMALL,
        name="grad_h_one",
    )(lax.axis_index("mp").reshape(1), a, b, parts)


def term_sum(refs):
    return functools.reduce(lambda total, ref: total + ref[...].astype(f32), refs[1:], refs[0][...].astype(f32))


def back_two_kernel(rank_ref, segment_ref, table_ref, *refs, width_mp, items):
    term_refs, (x_ref, attn_ref, cot_ref, proj_ref) = refs[:width_mp], refs[width_mp:-4]
    grad_x_ref, grad_attn_ref, grad_mixed_ref, sums_ref = refs[-4:]
    segment = segment_ref[...]
    width = x_ref.shape[1]
    heads = proj_ref.shape[0] // width_mp
    grad = term_sum(term_refs)
    normed, inverse = norm_parts(x_ref[...])
    scale = item_rows(table_ref, 4, width, segment, items)
    grad_x = cot_ref[...].astype(f32) + norm_back(normed, inverse, grad * (1.0 + scale))
    grad_x_ref[...] = grad_x
    grad_attn = (item_rows(table_ref, 2, width, segment, items) * grad_x).astype(bf16)
    grad_attn_ref[...] = grad_attn
    for place in range(width_mp):
        owner = lax.rem(rank_ref[0] - place + width_mp, width_mp)
        part = dot(proj_ref[place * heads : (place + 1) * heads, :], grad_attn, NT)
        grad_mixed_ref[owner] = part.astype(bf16)
    sums_ref[:, 0:width] = item_sums(grad_x * attn_ref[...], segment, items)
    sums_ref[:, width : 2 * width] = item_sums(grad, segment, items)
    sums_ref[:, 2 * width :] = item_sums(grad * normed, segment, items)


def back_two(terms, x_one, attn, cotangent, proj, table, segment):
    rows, width = x_one.shape
    items, width_mp = table.shape[0], lax.axis_size("mp")
    shapes = (
        jax.ShapeDtypeStruct((rows, width), f32),
        jax.ShapeDtypeStruct((rows, width), bf16),
        jax.ShapeDtypeStruct((width_mp, proj.shape[0] // width_mp, rows), bf16),
        jax.ShapeDtypeStruct((items, 3 * width), f32),
    )
    operands = (segment, table, *(t for t in terms), x_one, attn, cotangent, proj)
    return pl.pallas_call(
        functools.partial(back_two_kernel, width_mp=width_mp, items=items),
        out_shape=shapes,
        grid_spec=pltpu.PrefetchScalarGridSpec(
            num_scalar_prefetch=1,
            grid=(1,),
            in_specs=[plain(*o.shape) for o in operands],
            out_specs=tuple(plain(*o.shape) for o in shapes),
        ),
        compiler_params=pltpu.CompilerParams(vmem_limit_bytes=VMEM),
        cost_estimate=SMALL,
        name="back_two",
    )(lax.axis_index("mp").reshape(1), *operands)


def back_one_kernel(segment_ref, table_ref, *refs, items):
    term_refs, (patches_ref, grad_x_ref, grad_ref, sums_ref) = refs[:-4], refs[-4:]
    segment = segment_ref[...]
    width = patches_ref.shape[1]
    grad = term_sum(term_refs)
    normed, inverse = norm_parts(patches_ref[...].astype(f32))
    scale = item_rows(table_ref, 1, width, segment, items)
    grad_ref[...] = (grad_x_ref[...] + norm_back(normed, inverse, grad * (1.0 + scale))).astype(bf16)
    sums_ref[:, 0:width] = item_sums(grad, segment, items)
    sums_ref[:, width:] = item_sums(grad * normed, segment, items)


def outcome_kernel(segment_ref, table_ref, *refs, items):
    term_refs, (x_ref, cot_ref, out_ref, sums_ref) = refs[:-4], refs[-4:]
    segment = segment_ref[...]
    width = x_ref.shape[1]
    branch = term_sum(term_refs)
    gate = item_rows(table_ref, 5, width, segment, items)
    out_ref[...] = (x_ref[...] + gate * branch).astype(bf16)
    sums_ref[...] = item_sums(cot_ref[...].astype(f32) * branch, segment, items)


def own_rows(kernel, terms, first, second, table, segment, sums, name):
    rows, width = first.shape
    items = table.shape[0]
    shapes = (
        jax.ShapeDtypeStruct((rows, width), bf16),
        jax.ShapeDtypeStruct((items, sums * width), f32),
    )

    def single(*shape):
        return pl.BlockSpec(shape, lambda i: (0,) * len(shape))

    return pl.pallas_call(
        functools.partial(kernel, items=items),
        out_shape=shapes,
        grid=(1,),
        in_specs=[single(*segment.shape), single(*table.shape)]
        + [single(rows, width)] * (len(terms) + 2),
        out_specs=tuple(single(*o.shape) for o in shapes),
        compiler_params=pltpu.CompilerParams(vmem_limit_bytes=VMEM),
        cost_estimate=SMALL,
        name=name,
    )(segment, table, *terms, first, second)


def gelu_terms(before):
    slope = (2.0 / math.pi) ** 0.5
    square = before * before
    curve = jnp.tanh(slope * before * (1.0 + 0.044715 * square))
    half = 0.5 * (1.0 + curve)
    value = before * half
    derivative = half + (0.5 * slope) * before * (1.0 - curve * curve) * (1.0 + 0.134145 * square)
    return value, derivative


def slot_picks(place_row, capacity):
    slots = lax.broadcasted_iota(jnp.int32, (capacity, place_row.shape[1]), 0)
    return slots == place_row


def row_chunks(group):
    return [slice(first, first + 512) for first in range(0, group, 512)]


def before_kernel(
    place_ref, named_ref, branch_ref, weight_ref, *refs, count, shared
):
    slots_ref, named_slots_ref, back_ref = refs[-4:-1] if shared else refs[-3:]
    step = pl.program_id(0)

    @pl.when(step < count)
    def _():
        picks = slot_picks(place_ref[0], slots_ref.shape[1]).astype(bf16)
        slots = dot(picks, branch_ref[...]).astype(bf16)
        slots_ref[0] = slots
        named_slots_ref[0] = dot(picks, named_ref[...]).astype(bf16)
        back_ref[0] = dot(slots, weight_ref[0]).astype(bf16)

    if shared:

        @pl.when(step == count)
        def _():
            for chunk in row_chunks(branch_ref.shape[0]):
                refs[-1][chunk, :] = dot(branch_ref[chunk, :], weight_ref[0]).astype(bf16)


def whole(*shape):
    return pl.BlockSpec(shape, lambda *_: (0,) * len(shape), pipeline_mode=pl.Buffered(1))


def per_expert(experts, *shape):
    return pl.BlockSpec(
        (1,) + shape, lambda e, *_: (jnp.minimum(e, experts - 1),) + (0,) * len(shape)
    )


def per_slab(experts, *shape):
    return pl.BlockSpec((1,) + shape, lambda e, *_: (jnp.minimum(e, experts),) + (0,) * len(shape))


def experts_before(places, named, branch, out_t, capacity, first, held=None):
    group, width = branch.shape
    experts, hidden = out_t.shape[0] - 1, out_t.shape[2]
    base, count = (0, first) if held is None else (first, experts - first)
    shapes = (
        jax.ShapeDtypeStruct((experts, capacity, width), bf16),
        jax.ShapeDtypeStruct((experts, capacity, LANES), bf16),
        jax.ShapeDtypeStruct((experts, capacity, hidden), bf16),
    )

    def mine(*shape):
        return pl.BlockSpec(
            (1,) + shape, lambda e: (base + jnp.minimum(e, count - 1),) + (0,) * len(shape)
        )

    shared = held is not None
    return pl.pallas_call(
        functools.partial(before_kernel, count=count, shared=shared),
        out_shape=shapes + (jax.ShapeDtypeStruct((group, hidden), bf16),) * shared,
        grid=(count + shared,),
        in_specs=[
            mine(1, group),
            whole(group, LANES),
            whole(group, width),
            pl.BlockSpec((1, width, hidden), lambda e: (base + e, 0, 0)),
        ]
        + [pl.BlockSpec(memory_space=pl.ANY)] * (3 * shared),
        out_specs=(mine(capacity, width), mine(capacity, LANES), mine(capacity, hidden))
        + (whole(group, hidden),) * shared,
        input_output_aliases={4: 0, 5: 1, 6: 2} if shared else {},
        compiler_params=pltpu.CompilerParams(vmem_limit_bytes=VMEM),
        cost_estimate=SMALL,
        name="experts_before",
    )(places.reshape(experts, 1, group), named, branch, out_t, *(held or ()))


def slots_of(picked, slots):
    index = lax.broadcasted_iota(jnp.int32, (picked.shape[0], slots), 1)
    return ((index == picked[:, 0:1]) | (index == picked[:, 1:2])).astype(bf16)


def experts_kernel(
    rank_ref,
    place_ref,
    places_ref,
    picked_ref,
    rows_ref,
    weight_ref,
    router_ref,
    router_wide_ref,
    slots_ref,
    named_ref,
    back_ref,
    shared_back_ref,
    dispatched_ref,
    act_ref,
    grad_pre_ref,
    grad_res_ref,
    gate_ref,
    shared_act_ref,
    shared_grad_ref,
    grad_logits_ref,
    grad_rows_ref,
    grad_gates_ref,
    grad_slots_ref,
    high_ref,
    rest_ref,
    *,
    experts,
):
    step = pl.program_id(0)
    group = rows_ref.shape[0]
    capacity = slots_ref.shape[1]

    @pl.when(step < experts)
    def _():
        picks = slot_picks(place_ref[0], capacity)
        dispatched = dot(picks.astype(bf16), rows_ref[...]).astype(bf16)
        dispatched_ref[0] = dispatched
        pre = dot(dispatched, weight_ref[0])
        logits = dot(dispatched, router_wide_ref[...])
        lane = lax.broadcasted_iota(jnp.int32, logits.shape, 1)
        named = named_ref[0].astype(f32) > 0.0
        peak = jnp.max(jnp.where(named, logits, -jnp.inf), axis=1, keepdims=True)
        shares = jnp.where(named, jnp.exp(logits - peak), 0.0)
        total = jnp.sum(shares, axis=1, keepdims=True)
        own = jnp.sum(jnp.where(lane == step, shares, 0.0), axis=1, keepdims=True)
        gate = jnp.where(total > 0.0, own / jnp.maximum(total, 1.0), 0.0)
        gate_ref[0] = gate
        value, slope = gelu_terms(pre)
        act = value.astype(bf16)
        act_ref[0] = act
        back = back_ref[0].astype(f32)
        grad_pre = (gate * back * slope).astype(bf16)
        grad_pre_ref[0] = grad_pre
        grad_res_ref[0] = (gate * slots_ref[0].astype(f32)).astype(bf16)
        grad_gate = jnp.sum(back * act.astype(f32), axis=1, keepdims=True)
        grad_gates_ref[step] = jnp.sum(jnp.where(picks, grad_gate, 0.0), axis=0, keepdims=True)
        here = pl.ds(pl.multiple_of(step * capacity, capacity), capacity)
        grad_slots_ref[here, :] = dot(grad_pre, weight_ref[0], NT).astype(bf16)

    @pl.when(step == experts)
    def _():
        logits = dot(router_ref[...], rows_ref[...], NT)
        named = places_ref[...] >= 0
        peak = jnp.max(jnp.where(named, logits, -jnp.inf), axis=0, keepdims=True)
        shares = jnp.where(named, jnp.exp(logits - peak), 0.0)
        gates = shares / jnp.sum(shares, axis=0, keepdims=True)
        grad_gates = jnp.concatenate([grad_gates_ref[e] for e in range(experts)], axis=0)
        grad_logits = gates * (grad_gates - jnp.sum(gates * grad_gates, axis=0, keepdims=True))
        grad_logits_ref[...] = grad_logits
        high = grad_logits.astype(bf16)
        high_ref[...] = high
        rest_ref[...] = (grad_logits - high.astype(f32)).astype(bf16)

    @pl.when(step >= experts)
    def _():
        size = shared_act_ref.shape[0]
        here = pl.ds(pl.multiple_of((step - experts) * size, size), size)
        value, slope = gelu_terms(dot(rows_ref[here, :], weight_ref[0]))
        shared_act_ref[...] = value.astype(bf16)
        grad_pre = (shared_back_ref[...].astype(f32) * slope).astype(bf16)
        shared_grad_ref[...] = grad_pre
        total = dot(slots_of(picked_ref[...], experts * capacity), grad_slots_ref[...])
        total += dot(grad_pre, weight_ref[0], NT)
        total += dot(high_ref[:, here], router_ref[...], TN)
        total += dot(rest_ref[:, here], router_ref[...], TN)
        grad_rows_ref[...] = total.astype(bf16)


def row_block(experts, *shape):
    return pl.BlockSpec(shape, lambda e, *_: (jnp.maximum(e - experts, 0), 0))


def ring_block(experts, width_mp, *shape):
    def index(e, rank):
        return (lax.rem(rank[0] - jnp.maximum(e - experts, 0) + width_mp, width_mp), 0)

    return pl.BlockSpec(shape, index)


def experts_main(places, picked, h_two, in_w, router, slots, named, back, shared_back):
    group, width = h_two.shape
    experts, capacity, hidden = back.shape
    width_mp = lax.axis_size("mp")
    rows = group // width_mp
    slot_shape = jax.ShapeDtypeStruct((experts, capacity, width), bf16)
    unit_shape = jax.ShapeDtypeStruct((experts, capacity, hidden), bf16)
    return pl.pallas_call(
        functools.partial(experts_kernel, experts=experts),
        out_shape=(
            slot_shape,
            unit_shape,
            unit_shape,
            slot_shape,
            jax.ShapeDtypeStruct((experts, capacity, 1), f32),
            jax.ShapeDtypeStruct((group, hidden), bf16),
            jax.ShapeDtypeStruct((group, hidden), bf16),
            jax.ShapeDtypeStruct((experts, group), f32),
            jax.ShapeDtypeStruct((group, width), bf16),
        ),
        grid_spec=pltpu.PrefetchScalarGridSpec(
            num_scalar_prefetch=1,
            grid=(experts + width_mp,),
            in_specs=[
                per_expert(experts, 1, group),
                whole(experts, group),
                row_block(experts, rows, 2),
                whole(group, width),
                per_slab(experts, width, hidden),
                whole(experts, width),
                whole(width, LANES),
                per_expert(experts, capacity, width),
                per_expert(experts, capacity, LANES),
                per_expert(experts, capacity, hidden),
                row_block(experts, rows, hidden),
            ],
            out_specs=(
                per_expert(experts, capacity, width),
                per_expert(experts, capacity, hidden),
                per_expert(experts, capacity, hidden),
                per_expert(experts, capacity, width),
                per_expert(experts, capacity, 1),
                row_block(experts, rows, hidden),
                row_block(experts, rows, hidden),
                whole(experts, group),
                ring_block(experts, width_mp, rows, width),
            ),
            scratch_shapes=[
                pltpu.VMEM((experts, 1, group), f32),
                pltpu.VMEM((experts * capacity, width), bf16),
                pltpu.VMEM((experts, group), bf16),
                pltpu.VMEM((experts, group), bf16),
            ],
        ),
        compiler_params=pltpu.CompilerParams(vmem_limit_bytes=VMEM),
        cost_estimate=SMALL,
        name="experts_main",
    )(
        lax.axis_index("mp").reshape(1),
        places.reshape(experts, 1, group),
        places,
        picked,
        h_two,
        in_w,
        router.T,
        jnp.pad(router, ((0, 0), (0, LANES - experts))),
        slots,
        named,
        back,
        shared_back,
    )


def slab_kernel(a_ref, b_ref, a_shared_ref, b_shared_ref, out_ref, *, experts):
    step = pl.program_id(0)

    @pl.when(step < experts)
    def _():
        out_ref[0] = dot(a_ref[0], b_ref[0], TN).astype(bf16)

    @pl.when(step == experts)
    def _():
        out_ref[0] = dot(a_shared_ref[...], b_shared_ref[...], TN).astype(bf16)


def slab_product(a, b, a_shared, b_shared, name):
    experts, capacity, width = a.shape
    hidden = b.shape[2]
    group = a_shared.shape[0]
    return pl.pallas_call(
        functools.partial(slab_kernel, experts=experts),
        out_shape=jax.ShapeDtypeStruct((experts + 1, width, hidden), bf16),
        grid=(experts + 1,),
        in_specs=[
            per_expert(experts, capacity, width),
            per_expert(experts, capacity, hidden),
            whole(group, width),
            whole(group, hidden),
        ],
        out_specs=per_slab(experts, width, hidden),
        compiler_params=pltpu.CompilerParams(vmem_limit_bytes=VMEM),
        cost_estimate=SMALL,
        name=name,
    )(a, b, a_shared, b_shared)


def branch_kernel(
    rank_ref, picked_ref, gate_ref, act_ref, weight_ref, shared_ref, out_ref, res_ref, *, experts
):
    step = pl.program_id(0)
    capacity = act_ref.shape[1]

    @pl.when(step < experts)
    def _():
        here = pl.ds(pl.multiple_of(step * capacity, capacity), capacity)
        res_ref[here, :] = (gate_ref[0] * dot(act_ref[0], weight_ref[0], NT)).astype(bf16)

    @pl.when(step >= experts)
    def _():
        total = dot(slots_of(picked_ref[...], experts * capacity), res_ref[...])
        out_ref[...] = (total + dot(shared_ref[...], weight_ref[0], NT)).astype(bf16)


def experts_out(picked, gates, act, out_t, shared_act):
    experts, capacity, hidden = act.shape
    group, width, width_mp = shared_act.shape[0], out_t.shape[1], lax.axis_size("mp")
    rows = group // width_mp
    return pl.pallas_call(
        functools.partial(branch_kernel, experts=experts),
        out_shape=jax.ShapeDtypeStruct((group, width), bf16),
        grid_spec=pltpu.PrefetchScalarGridSpec(
            num_scalar_prefetch=1,
            grid=(experts + width_mp,),
            in_specs=[
                row_block(experts, rows, 2),
                per_expert(experts, capacity, 1),
                per_expert(experts, capacity, hidden),
                per_slab(experts, width, hidden),
                row_block(experts, rows, hidden),
            ],
            out_specs=ring_block(experts, width_mp, rows, width),
            scratch_shapes=[pltpu.VMEM((experts * capacity, width), bf16)],
        ),
        compiler_params=pltpu.CompilerParams(vmem_limit_bytes=VMEM),
        cost_estimate=SMALL,
        name="experts_out",
    )(lax.axis_index("mp").reshape(1), picked, gates, act, out_t, shared_act)


def adamw_update(master, first, second, gradient, fan_in):
    step_rate = 0.5 * fan_in ** (-0.5)
    first_new = beta_one * first + (1.0 - beta_one) * gradient
    second_new = beta_two * second + (1.0 - beta_two) * gradient * gradient
    first_hat = first_new / (1.0 - beta_one**STEP)
    second_hat = second_new / (1.0 - beta_two**STEP)
    master_new = master - step_rate * (
        first_hat / (jnp.sqrt(second_hat) + epsilon) + weight_decay * master
    )
    return (master_new, first_new, second_new, master_new.astype(bf16))


def body(
    patches,
    cotangent,
    conditioning,
    lengths,
    routes,
    ada_weight,
    ada_first,
    ada_second,
    router_weight,
    router_first,
    router_second,
    qkv_weight,
    qkv_first,
    qkv_second,
    proj_weight,
    proj_first,
    proj_second,
    shared_in_weight,
    shared_in_first,
    shared_in_second,
    shared_out_weight,
    shared_out_first,
    shared_out_second,
    expert_in_weight,
    expert_in_first,
    expert_in_second,
    expert_out_weight,
    expert_out_first,
    expert_out_second,
):
    rows, D = patches.shape
    width = lax.axis_size("mp")
    n_dp = lax.axis_size("dp")
    devices = width * n_dp
    group = rows * width
    capacity = 5 * group // 16
    heads_here = H // width
    model_rank = lax.axis_index("mp")
    item_count = lengths.shape[1]
    hidden = shared_in_weight.shape[1]
    ada_cols = ada_weight.shape[1]
    router_cols = router_weight.shape[0]

    out_slab = jnp.concatenate(
        [
            jnp.swapaxes(expert_out_weight.astype(bf16), 1, 2),
            shared_out_weight.astype(bf16).T[None],
        ],
        axis=0,
    )
    in_slab = jnp.concatenate(
        [expert_in_weight.astype(bf16), shared_in_weight.astype(bf16)[None]], axis=0
    )
    out_t = lax.all_gather(out_slab, "dp", axis=1, tiled=True)
    proj_block = proj_weight.astype(bf16).T
    proj_shape = proj_block.shape
    proj_rows = proj_block.size // D
    fill = -proj_rows % 32

    def riding(blocks):
        return jnp.pad(blocks, ((0, 0),) * (blocks.ndim - 2) + ((0, fill), (0, 0)))

    patches_blocks = ring_gather(
        after(jnp.concatenate([patches, riding(proj_block.reshape(-1, D))], axis=0), out_slab)
    )

    def over_dp(values):
        parts = lax.all_to_all(
            values.reshape((n_dp, values.shape[0] // n_dp) + values.shape[1:]), "dp", 0, 0, tiled=True
        )
        return jnp.sum(parts.astype(f32), axis=0)

    def from_dp(values):
        parts = jnp.broadcast_to(values[None], (n_dp,) + values.shape)
        return lax.all_to_all(parts, "dp", 0, 0, tiled=True).reshape((-1,) + values.shape[1:])

    cond_all = lax.all_gather(conditioning, "dp", axis=0, tiled=True)
    cond_act = jax.nn.silu(cond_all.astype(f32)).astype(bf16)
    columns = jnp.dot(cond_act, ada_weight.astype(bf16), preferred_element_type=f32)
    columns = jnp.repeat(columns.reshape(n_dp, item_count * ada_cols), width, axis=0)
    router_low = router_weight.astype(bf16).astype(f32)
    payload = jnp.concatenate(
        [columns, jnp.broadcast_to(router_low[None], (devices, router_cols))], axis=1
    )
    received = lax.all_to_all(payload, ("dp", "mp"), 0, 0, tiled=True)
    qkv_here = lax.all_gather(
        after(qkv_weight.astype(bf16), cond_all), "dp", axis=0, tiled=True
    )
    modulation = (
        received[:, : item_count * ada_cols]
        .reshape(devices, item_count, ada_cols)
        .transpose(1, 0, 2)
        .reshape(item_count, devices * ada_cols)
    )
    router_matrix = received[:, item_count * ada_cols :].reshape(D, E).astype(bf16)
    bounds = jnp.cumsum(lengths[0])
    places = jnp.arange(group, dtype=jnp.int32)
    segment = jnp.sum((places[:, None] >= bounds[None, :]).astype(jnp.int32), axis=1)
    segment_column = segment[:, None]
    segment_mine = lax.dynamic_slice_in_dim(segment_column, model_rank * rows, rows, 0)
    start, kind = key_windows(lengths[0], group)

    chosen = routes[:, :, None] == jnp.arange(E, dtype=jnp.int32)[None, None, :]
    names = chosen.any(axis=1)
    below = (places[:, None] > places[None, :]).astype(bf16)
    earlier = jnp.dot(below, names.astype(bf16), preferred_element_type=f32).astype(jnp.int32)
    place_of = jnp.where(names, earlier, -1).T
    picked = routes * capacity + jnp.sum(jnp.where(chosen, earlier[:, None, :], 0), axis=2)
    names_low = jnp.pad(names.astype(bf16), ((0, 0), (0, LANES - E)))

    cot_blocks = ring_gather(after(cotangent, *patches_blocks))
    patches_all, h_one_all, qkv, qkv_wide = norm_one(
        patches_blocks, rows, modulation, segment_column, qkv_here
    )
    proj_here = jnp.concatenate(
        [b[rows : rows + proj_rows].reshape(proj_shape) for b in patches_blocks], axis=1
    )
    qkv, out_t = lax.optimization_barrier((qkv, out_t))
    in_w = lax.all_gather(after(in_slab, out_t), "dp", axis=1, tiled=True)
    proj_t = from_dp(after(proj_here, qkv))
    near, far = (1, width - 1), tuple(range(2, width - 1))
    mixed_here, logs, cot_near = lax.optimization_barrier(
        (*attend(qkv, start, kind), [cot_blocks[i] for i in near])
    )
    cot_near = dict(zip(near, cot_near))
    cot_blocks = [cot_near.get(i, block) for i, block in enumerate(cot_blocks)]
    mixed_blocks = ring_gather(mixed_here)
    (grad_branch,) = by_rows(
        gated_kernel,
        1,
        after(cot_blocks, mixed_here),
        rows,
        modulation,
        segment_column,
        "grad_branch",
    )
    held = experts_before(place_of, names_low, grad_branch, out_t, capacity, E // 2)
    held = experts_before(place_of, names_low, grad_branch, out_t, capacity, E // 2, held)
    mixed_blocks, held, proj_t = lax.optimization_barrier((mixed_blocks, held, proj_t))
    branch_slots, named_slots, back_slots, back_shared = held
    h_two, x_one_mine, attn_mine, mixed_mine, proj = norm_two(
        mixed_blocks, patches_all, proj_t, modulation, segment_column
    )

    (
        dispatched,
        expert_act,
        grad_expert_pre,
        grad_res,
        gates,
        shared_act,
        grad_shared_pre,
        grad_logits,
        grad_h_two,
    ) = experts_main(
        place_of,
        picked,
        h_two,
        in_w,
        router_matrix,
        branch_slots,
        named_slots,
        back_slots,
        back_shared,
    )
    two_terms = ring_scatter(grad_h_two)

    two_terms, grad_out_slab, mlp_part = sent_beside(
        two_terms,
        slab_product(grad_res, expert_act, grad_branch, shared_act, "grad_out"),
        lambda near: experts_out(picked, after(gates, near), expert_act, out_t, shared_act),
    )
    grad_out_mine = lax.psum_scatter(grad_out_slab, "dp", scatter_dimension=1, tiled=True)
    grad_x_one, grad_attn, grad_mixed_mine, sums_two = back_two(
        two_terms, x_one_mine, attn_mine, cotangent, proj, modulation, segment_mine
    )
    grad_mixed = lax.all_to_all(grad_mixed_mine, "mp", 0, 0, tiled=True)
    mlp_terms = ring_scatter(mlp_part)
    grad_in_slab = slab_product(
        after(dispatched, grad_mixed_mine), grad_expert_pre, h_two, grad_shared_pre, "grad_in"
    )
    grad_router = jnp.einsum(
        "gd,eg->de", h_two.astype(f32), after(grad_logits, grad_mixed_mine), precision=highest
    )
    grad_mixed, grad_router, grad_in_slab, mlp_near, grad_out_mine = lax.optimization_barrier(
        (grad_mixed, grad_router, grad_in_slab, [mlp_terms[i] for i in near], grad_out_mine)
    )
    grad_in_mine = lax.psum_scatter(
        after(grad_in_slab, grad_out_mine), "dp", scatter_dimension=1, tiled=True
    )
    grad_mixed = grad_mixed.transpose(1, 0, 2).reshape(heads_here * HD, group)
    grad_proj_t = jnp.einsum(
        "gd,cg->dc", after(grad_attn, grad_mixed), mixed_mine, preferred_element_type=f32
    )
    grad_proj_t = over_dp(grad_proj_t.astype(bf16)).astype(bf16)
    grad_qkv, grad_proj_t, mlp_far = lax.optimization_barrier(
        (
            attend_back(qkv, grad_mixed, logs, start, kind),
            grad_proj_t,
            [mlp_terms[i] for i in far],
        )
    )
    proj_parts = grad_proj_t.reshape(proj_shape[0], width, proj_shape[1]).transpose(1, 0, 2)
    partial = ring_product(grad_qkv, qkv_wide, riding(proj_parts.reshape(width, -1, D)))
    one_terms = ring_scatter(partial)
    grad_qkv = after(grad_qkv, partial)
    grad_qkv_weight = jnp.einsum("gd,gc->dc", h_one_all, grad_qkv, preferred_element_type=f32)
    grad_qkv_weight = grad_qkv_weight.reshape(D, heads_here * 3, LANES)[:, :, :HD]
    grad_qkv_weight = grad_qkv_weight.reshape(D, heads_here * 3 * HD).astype(bf16)
    one_terms, grad_qkv_weight, (result, sums_gate, grad_qkv_mine, grad_in_mine) = sent_beside(
        one_terms,
        grad_qkv_weight,
        lambda made: (
            *own_rows(
                outcome_kernel,
                after([mlp_terms[0], *mlp_near, *mlp_far], made),
                x_one_mine,
                cotangent,
                modulation,
                segment_mine,
                1,
                "outcome",
            ),
            over_dp(made),
            grad_in_mine,
        ),
    )
    patch_grad, sums_one = own_rows(
        back_one_kernel, one_terms, patches, grad_x_one, modulation, segment_mine, 2, "back_one"
    )
    grad_proj_mine = sum(
        t[rows : rows + proj_rows].astype(f32) for t in one_terms
    ).reshape(proj_shape)
    grad_modulation = jnp.concatenate([sums_one, sums_two, sums_gate], axis=1)
    payload = jnp.concatenate(
        [
            grad_modulation.reshape(item_count, devices, ada_cols)
            .transpose(1, 0, 2)
            .reshape(devices, item_count * ada_cols),
            grad_router.reshape(devices, router_cols),
        ],
        axis=1,
    )
    received = lax.all_to_all(payload, ("dp", "mp"), 0, 0, tiled=True)
    router_grad = jnp.sum(received[:, item_count * ada_cols :], axis=0)
    columns = jnp.sum(
        received[:, : item_count * ada_cols].reshape(n_dp, width, item_count, ada_cols), axis=1
    ).reshape(n_dp * item_count, ada_cols)
    ada_grad = jnp.einsum("id,ic->dc", cond_act.astype(f32), columns, precision=highest)
    grad_out_mine, grad_in_mine = grad_out_mine.astype(f32), grad_in_mine.astype(f32)

    gradients = (
        ada_grad,
        router_grad,
        grad_qkv_mine,
        grad_proj_mine.T,
        grad_in_mine[E],
        grad_out_mine[E].T,
        grad_in_mine[:E],
        jnp.swapaxes(grad_out_mine[:E], 1, 2),
    )
    states_of = (
        (ada_weight, ada_first, ada_second),
        (router_weight, router_first, router_second),
        (qkv_weight, qkv_first, qkv_second),
        (proj_weight, proj_first, proj_second),
        (shared_in_weight, shared_in_first, shared_in_second),
        (shared_out_weight, shared_out_first, shared_out_second),
        (expert_in_weight, expert_in_first, expert_in_second),
        (expert_out_weight, expert_out_first, expert_out_second),
    )
    total_hidden = float(hidden * width)
    fan_ins = (D, D, D, 8.0 * D / group, D, total_hidden, D, total_hidden)
    updates = []
    for (master, first, second), gradient, fan_in in zip(states_of, gradients, fan_ins):
        updates.extend(adamw_update(master, first, second, gradient, float(fan_in)))
    return tuple([result, patch_grad] + updates)


def solution(mesh):
    tokens, data = P(("dp", "mp"), None), P("dp", None)
    ada, router = P(None, ("dp", "mp")), P(("dp", "mp"))
    deep, wide = P("dp", "mp"), P("mp", "dp")
    deep_experts, wide_experts = P(None, "dp", "mp"), P(None, "mp", "dp")
    kinds = (ada, router, deep, wide, deep, wide, deep_experts, wide_experts)
    in_specs = (tokens, tokens, data, data, data) + tuple(k for k in kinds for _ in range(3))
    out_specs = (tokens, tokens) + tuple(k for k in kinds for _ in range(4))
    return jax.shard_map(body, mesh=mesh, in_specs=in_specs, out_specs=out_specs, check_vma=False)
```

profile of v0, /device:TPU:0, one launch (start us, length us, event | category | flops | bytes accessed | tf_op | source)
XLA Modules:
  0.0 534.9 jit_solution(18219661502966243166)
XLA Ops:
  17.8 10.1 %all-gather = bf16[8,3,768]{2,1,0:T(4,128)(2,1)} all-gather(bf16[1,3,768]{2,1,0:T(4,128)(2,1)S(1)} %bitcast.106), channel_id=1, replica_groups=mesh['dp'=8,'mp'=4] {'dp'}, dimensions={0}, use_global_device_ids=true | all-gather | bytes 41472 | tf_op jit(solution)/shard_map/all_gather | solution.py:966
  41.2 17.9 %all_gather.13.refs_4_ = bf16[768,576]{1,0:T(8,128)(2,1)} all-gather(bf16[96,576]{1,0:T(8,128)(2,1)} %convert_element_type.122), channel_id=1, replica_groups=mesh['dp'=8,'mp'=4] {'dp'}, dimensions={0}, use_global_device_ids=true | all-gather | bytes 995328 | tf_op jit(solution)/shard_map/all_gather | solution.py:975
  61.7 13.0 %all-to-all-done = f32[32,1,624]{2,1,0:T(1,128)} async-done(((f32[32,1,624]{2,1,0:T(1,128)}), f32[32,1,624]{2,1,0:T(1,128)}, u32[]{:S(2)}, u32[]{:S(2)}) %all-to-all-start) | async-done | bytes 79904 | tf_op jit(solution)/shard_map/all_to_all | solution.py:974
  76.5 10.2 %norm_one.1 = (bf16[1536,768]{1,0:T(8,128)(2,1)}, bf16[1536,768]{1,0:T(8,128)(2,1)}, bf16[1536,1152]{1,0:T(8,128)(2,1)}, bf16[768,1152]{1,0:T(8,128)(2,1)}) custom-call(s32[1]{0:T(128)} %bitcast.refs_0_.rank_ref, s32[1536,1]{1,0:T(8,128)} %broadcast_in_dim.83.refs_1_, f32[3,4608]{1,0:T(4,128)} %reshape.220.refs_2_.table_ref, ...), custom_call_target="tpu_custom_call" | custom-call | flops 1000000 | bytes 100000 | tf_op jit(solution)/shard_map/norm_one/pallas_call | solution.py:273
  103.1 20.1 %attend.1 = (bf16[192,1536]{1,0:T(8,128)(2,1)}, f32[3,1,1536]{2,1,0:T(1,128)}) custom-call(s32[6]{0:T(128)} %subtract_minimum_fusion.start_ref, s32[6]{0:T(128)} %copy-done.40, bf16[1536,1152]{1,0:T(8,128)(2,1)} %get-tuple-element.128.qkv_ref), custom_call_target="tpu_custom_call" | custom-call | flops 1000000 | bytes 100000 | tf_op jit(solution)/shard_map/attend/pallas_call | solution.py:125
  133.1 36.0 %collective-permute-done.8.refs_5_ = bf16[384,768]{1,0:T(8,128)(2,1)} collective-permute-done((bf16[384,768]{1,0:T(8,128)(2,1)S(1)}, bf16[384,768]{1,0:T(8,128)(2,1)}, u32[]{:S(2)}, u32[]{:S(2)}) %collective-permute-start.8) | collective-permute-done | bytes 589856 | tf_op jit(solution)/shard_map/ppermute | solution.py:46
  169.1 5.0 grad_branch.1.branch_ref.a_shared_ref
  174.1 12.6 %experts_before.2 = (bf16[8,480,768]{2,1,0:T(8,128)(2,1)}, bf16[8,480,128]{2,1,0:T(8,128)(2,1)}, bf16[8,480,768]{2,1,0:T(8,128)(2,1)}) custom-call(s32[8,1,1536]{2,1,0:T(1,128)} %copy.189.place_ref, bf16[1536,128]{1,0:T(8,128)(2,1)} %pad_convert_fusion.named_ref, bf16[1536,768]{1,0:T(8,128)(2,1)} %grad_branch.1.branch_ref.a_shared_ref, ...), custom_call_target="tpu_custom_call" | custom-call | flops 1000000 | bytes 100000 | tf_op jit(solution)/shard_map/experts_before/pallas_call | solution.py:603
  186.7 15.5 %experts_before.3 = (bf16[8,480,768]{2,1,0:T(8,128)(2,1)}, bf16[8,480,128]{2,1,0:T(8,128)(2,1)}, bf16[8,480,768]{2,1,0:T(8,128)(2,1)}, bf16[1536,768]{1,0:T(8,128)(2,1)}) custom-call(s32[8,1,1536]{2,1,0:T(1,128)} %copy.189.place_ref, bf16[1536,128]{1,0:T(8,128)(2,1)} %pad_convert_fusion.named_ref, ...), custom_call_target="tpu_custom_call", output_to_operand_aliasing={{0}: (4, {}), {1}: (5, {}), {2}: (6, {})} | custom-call | flops 1000000 | bytes 100000 | tf_op jit(solution)/shard_map/experts_before/pallas_call | solution.py:603
  203.2 13.1 %norm_two.1 = (bf16[1536,768]{1,0:T(8,128)(2,1)}, f32[384,768]{1,0:T(8,128)}, f32[384,768]{1,0:T(8,128)}, bf16[768,384]{1,0:T(8,128)(2,1)}, bf16[768,768]{1,0:T(8,128)(2,1)}) custom-call(s32[1]{0:T(128)} %bitcast.refs_0_.rank_ref, s32[1536,1]{1,0:T(8,128)} %broadcast_in_dim.83.refs_1_, f32[3,4608]{1,0:T(4,128)} %reshape.220.refs_2_.table_ref, ...), custom_call_target="tpu_custom_call" | custom-call | flops 1000000 | bytes 100000 | tf_op jit(solution)/shard_map/norm_two/pallas_call | solution.py:373
  216.3 59.1 %experts_main.1 = (bf16[8,480,768]{2,1,0:T(8,128)(2,1)}, bf16[8,480,768]{2,1,0:T(8,128)(2,1)}, bf16[8,480,768]{2,1,0:T(8,128)(2,1)}, bf16[8,480,768]{2,1,0:T(8,1...) custom-call(s32[1]{0:T(128)} %bitcast.refs_0_.rank_ref, ...), custom_call_target="tpu_custom_call" | custom-call | flops 1000000 | bytes 100000 | tf_op jit(solution)/shard_map/experts_main/pallas_call | solution.py:735
  278.0 3.8 collective-permute-start.9
  281.8 16.0 %grad_out.1 = bf16[9,768,768]{2,1,0:T(8,128)(2,1)} custom-call(bf16[8,480,768]{2,1,0:T(8,128)(2,1)} %get-tuple-element.161.a_ref, bf16[8,480,768]{2,1,0:T(8,128)(2,1)} %get-tuple-element.162.b_ref.act_ref, bf16[1536,768]{1,0:T(8,128)(2,1)} %grad_branch.1.branch_ref.a_shared_ref, bf16[1536,768]{1,0:T(8,128)(2,1)} %get-tuple-element.163.b_shared_ref.shared_ref), custom_call_target="tpu_custom_call" | custom-call | flops 1000000 | bytes 100000 | tf_op jit(solution)/shard_map/grad_out/pallas_call | solution.py:817
  297.8 5.5 %collective-permute-done.9.refs_1_ = bf16[384,768]{1,0:T(8,128)(2,1)S(1)} collective-permute-done((bf16[384,768]{1,0:T(8,128)(2,1)S(1)}, bf16[384,768]{1,0:T(8,128)(2,1)S(1)}, u32[]{:S(2)}, u32[]{:S(2)}) %collective-permute-start.9) | collective-permute-done | bytes 589856 | tf_op jit(solution)/shard_map/ppermute | solution.py:66
  307.8 27.2 %experts_out.1 = bf16[1536,768]{1,0:T(8,128)(2,1)} custom-call(s32[1]{0:T(128)} %bitcast.refs_0_.rank_ref, s32[1536,2]{1,0:T(8,128)} %copy.190.picked_ref, f32[8,480,1]{2,1,0:T(8,128)} %get-tuple-element.167.gate_ref, bf16[8,480,768]{2,1,0:T(8,128)(2,1)} %get-tuple-element.162.b_ref.act_ref, bf16[9,768,768]{2,1,0:T(8,128)(2,1)} %all-gather.4.cloned.1.call-done.weight_ref, ...), custom_call_target="tpu_custom_call" | custom-call | flops 1000000 | bytes 100000 | tf_op jit(solution)/shard_map/experts_out/pallas_call | solution.py:855
  335.9 7.2 %back_two.1 = (f32[384,768]{1,0:T(8,128)}, bf16[384,768]{1,0:T(8,128)(2,1)}, bf16[4,192,384]{2,1,0:T(8,128)(2,1)}, f32[3,2304]{1,0:T(4,128)}) custom-call(s32[1]{0:T(128)} %bitcast.refs_0_.rank_ref, s32[384,1]{1,0:T(8,128)} %dynamic_slice.4.segment_ref, f32[3,4608]{1,0:T(4,128)} %reshape.220.refs_2_.table_ref, bf16[384,768]{1,0:T(8,128)(2,1)} %get-tuple-element.261.refs_0_, ...), custom_call_target="tpu_custom_call" | custom-call | flops 1000000 | bytes 100000 | tf_op jit(solution)/shard_map/back_two/pallas_call | solution.py:471
  348.0 3.7 collective-permute-start.12
  351.8 16.2 %grad_in.1 = bf16[9,768,768]{2,1,0:T(8,128)(2,1)} custom-call(bf16[8,480,768]{2,1,0:T(8,128)(2,1)} %get-tuple-element.177.a_ref, bf16[8,480,768]{2,1,0:T(8,128)(2,1)} %get-tuple-element.178.b_ref, bf16[1536,768]{1,0:T(8,128)(2,1)} %get-tuple-element.154.rows_ref.a_shared_ref, bf16[1536,768]{1,0:T(8,128)(2,1)} %get-tuple-element.179.b_shared_ref), custom_call_target="tpu_custom_call" | custom-call | flops 1000000 | bytes 100000 | tf_op jit(solution)/shard_map/grad_in/pallas_call | solution.py:817
  370.5 10.8 %collective-permute-done.13.refs_2_ = bf16[384,768]{1,0:T(8,128)(2,1)} collective-permute-done((bf16[384,768]{1,0:T(8,128)(2,1)}, bf16[384,768]{1,0:T(8,128)(2,1)}, u32[]{:S(2)}, u32[]{:S(2)}) %collective-permute-start.13) | collective-permute-done | bytes 589856 | tf_op jit(solution)/shard_map/ppermute | solution.py:66
  387.6 4.3 all-to-all-start.3
  396.0 25.2 %attend_back.1.a_ref = bf16[1536,1152]{1,0:T(8,128)(2,1)} custom-call(s32[6]{0:T(128)} %subtract_minimum_fusion.start_ref, s32[6]{0:T(128)} %copy-done.40, bf16[1536,1152]{1,0:T(8,128)(2,1)} %get-tuple-element.128.qkv_ref, bf16[192,1536]{1,0:T(8,128)(2,1)} %bitcast.96, f32[3,1,1536]{2,1,0:T(1,128)} %get-tuple-element.182.log_ref), custom_call_target="tpu_custom_call" | custom-call | flops 1000000 | bytes 100000 | tf_op jit(solution)/shard_map/attend_back/pallas_call | solution.py:187
  423.8 7.0 %grad_h_one.1 = bf16[1664,768]{1,0:T(8,128)(2,1)} custom-call(s32[1]{0:T(128)} %bitcast.refs_0_.rank_ref, bf16[1536,1152]{1,0:T(8,128)(2,1)} %attend_back.1.a_ref, bf16[768,1152]{1,0:T(8,128)(2,1)} %get-tuple-element.187.b_ref, bf16[4,32,768]{2,1,0:T(8,128)(2,1)} %pad.22.part_ref), custom_call_target="tpu_custom_call" | custom-call | flops 1000000 | bytes 100000 | tf_op jit(solution)/shard_map/grad_h_one/pallas_call | solution.py:416
  436.4 6.2 %convolution_convert_fusion = bf16[768,1152]{1,0:T(8,128)(2,1)} fusion(bf16[1536,768]{1,0:T(8,128)(2,1)} %get-tuple-element.192, bf16[1536,1152]{1,0:T(8,128)(2,1)S(1)} %copy-done.2), kind=kOutput, calls=%fused_computation.5 | convolution fusion | flops 2718793728 | bytes 7667712 | tf_op jit(solution)/shard_map/gd,gc->dc/dot_general | solution.py:1096
  442.7 3.9 copy.195
  451.2 14.5 %collective-permute-done.17.refs_3_ = bf16[416,768]{1,0:T(8,128)(2,1)} collective-permute-done((bf16[416,768]{1,0:T(8,128)(2,1)}, bf16[416,768]{1,0:T(8,128)(2,1)}, u32[]{:S(2)}, u32[]{:S(2)}) %collective-permute-start.17) | collective-permute-done | bytes 639008 | tf_op jit(solution)/shard_map/ppermute | solution.py:66
  467.0 4.2 all-to-all-start.4
  471.3 7.6 %fusion.26 = (bf16[8,768,96]{1,2,0:T(8,128)(2,1)}, f32[8,768,96]{1,2,0:T(8,128)}, f32[8,768,96]{1,2,0:T(8,128)}, f32[8,768,96]{1,2,0:T(8,128)}) fusion(f32[8,768,96]{1,2,0:T(8,128)} %param.57, f32[9,96,768]{2,1,0:T(8,128)S(1)} %convert_element_type.143, f32[8,768,96]{1,2,0:T(8,128)} %param.58, f32[8,768,96]{1,2,0:T(8,128)} %param.59), kind=kLoop, calls=%fused_computation.97 | loop fusion | flops 9437184 | bytes 17694720 | tf_op jit(solution)/shard_map/convert_element_type | solution.py:886
  481.5 3.7 outcome.1
  487.4 4.3 collective-permute-done.15.refs_2_
  494.3 4.7 back_one.1
  500.9 13.2 %all-to-all-start.5 = ((f32[32,1,624]{2,1,0:T(1,128)}), f32[32,1,624]{2,1,0:T(1,128)S(1)}, u32[]{:S(2)}, u32[]{:S(2)}) async-start(f32[32,1,624]{2,1,0:T(1,128)} %copy.201), calls=%async_computation.7 | async-start | bytes 163840 | tf_op jit(solution)/shard_map/all_to_all | solution.py:1133
  514.1 7.7 %fusion.28 = (bf16[8,96,768]{2,1,0:T(8,128)(2,1)}, f32[8,96,768]{2,1,0:T(8,128)}, f32[8,96,768]{2,1,0:T(8,128)}, f32[8,96,768]{2,1,0:T(8,128)}) fusion(f32[8,96,768]{2,1,0:T(8,128)} %param.54, f32[9,96,768]{2,1,0:T(8,128)S(1)} %convert_element_type.141, f32[8,96,768]{2,1,0:T(8,128)} %param.55, f32[8,96,768]{2,1,0:T(8,128)} %param.56), kind=kLoop, calls=%fused_computation.98 | loop fusion | flops 9437184 | bytes 17694720 | tf_op jit(solution)/shard_map/convert_element_type | solution.py:886
  (243 shorter events, 110.1 us)
Async XLA Ops:
  7.2 79.5 %all-gather.4.cloned.1.call-start = ((), (), s32[]{:S(2)}) async-start(), calls=%async_computation.8 | async-start | bytes 11943936 | tf_op jit(solution)/shard_map/all_gather | solution.py:943
  10.4 48.7 %copy-start.11 = (f32[96,768]{1,0:T(8,128)S(1)}, f32[96,768]{1,0:T(8,128)}, u32[]{:S(2)}) copy-start(f32[96,768]{1,0:T(8,128)} %param.48) | copy-start | bytes 884740
  10.7 49.8 %copy-start.7 = (bf16[416,768]{1,0:T(8,128)(2,1)}, bf16[416,768]{1,0:T(8,128)(2,1)S(1)}, u32[]{:S(2)}) copy-start(bf16[416,768]{1,0:T(8,128)(2,1)S(1)} %fusion.5.refs_5_) | copy-start | bytes 1916932
  10.7 49.6 %copy-start.3 = (f32[8,96,768]{2,1,0:T(8,128)S(1)}, f32[8,96,768]{2,1,0:T(8,128)}, u32[]{:S(2)}) copy-start(f32[8,96,768]{2,1,0:T(8,128)} %param.54) | copy-start | bytes 7077892
  10.7 65.7 %collective-permute-start = (bf16[416,768]{1,0:T(8,128)(2,1)S(1)}, bf16[416,768]{1,0:T(8,128)(2,1)}, u32[]{:S(2)}, u32[]{:S(2)}) collective-permute-start(bf16[416,768]{1,0:T(8,128)(2,1)S(1)} %fusion.5.refs_5_), channel_id=1, source_target_pairs={{0,1},{1,2},{2,3},{3,0},{4,5},{5,6},{6,7},{7,4},{8,9},{9,10},{10,1... | collective-permute-start | bytes 1916936 | tf_op jit(solution)/shard_map/ppermute | solution.py:46
  13.8 62.7 %collective-permute-start.1 = (bf16[416,768]{1,0:T(8,128)(2,1)S(1)}, bf16[416,768]{1,0:T(8,128)(2,1)}, u32[]{:S(2)}, u32[]{:S(2)}) collective-permute-start(bf16[416,768]{1,0:T(8,128)(2,1)S(1)} %fusion.5.refs_5_), channel_id=1, source_target_pairs={{0,2},{1,3},{2,0},{3,1},{4,6},{5,7},{6,4},{7,5},{8,10},{9,11},{10,... | collective-permute-start | bytes 1916936 | tf_op jit(solution)/shard_map/ppermute | solution.py:46
  16.4 60.1 %collective-permute-start.2 = (bf16[416,768]{1,0:T(8,128)(2,1)S(1)}, bf16[416,768]{1,0:T(8,128)(2,1)}, u32[]{:S(2)}, u32[]{:S(2)}) collective-permute-start(bf16[416,768]{1,0:T(8,128)(2,1)S(1)} %fusion.5.refs_5_), channel_id=1, source_target_pairs={{0,3},{1,0},{2,1},{3,2},{4,7},{5,4},{6,5},{7,6},{8,11},{9,8},{10,9... | collective-permute-start | bytes 1916936 | tf_op jit(solution)/shard_map/ppermute | solution.py:46
  36.4 38.3 %all-to-all-start = ((f32[32,1,624]{2,1,0:T(1,128)}), f32[32,1,624]{2,1,0:T(1,128)}, u32[]{:S(2)}, u32[]{:S(2)}) async-start(f32[32,1,624]{2,1,0:T(1,128)} %all_to_all.28), calls=%async_computation | async-start | bytes 163840 | tf_op jit(solution)/shard_map/all_to_all | solution.py:974
  39.7 176.7 %all-gather.6.cloned.1.call-start = ((), (), s32[]{:S(2)}) async-start(), calls=%async_computation.9 | async-start | bytes 11943936 | tf_op jit(solution)/shard_map/all_gather | solution.py:1008
  88.6 34.6 %collective-permute-start.3 = (bf16[384,768]{1,0:T(8,128)(2,1)S(1)}, bf16[384,768]{1,0:T(8,128)(2,1)S(1)}, u32[]{:S(2)}, u32[]{:S(2)}) collective-permute-start(bf16[384,768]{1,0:T(8,128)(2,1)S(1)} %copy-done.5), channel_id=1, source_target_pairs={{0,1},{1,2},{2,3},{3,0},{4,5},{5,6},{6,7},{7,4},{8,9},{9,10},{10,1... | collective-permute-start | bytes 1769480 | tf_op jit(solution)/shard_map/ppermute | solution.py:46
  89.5 33.7 %collective-permute-start.4 = (bf16[384,768]{1,0:T(8,128)(2,1)S(1)}, bf16[384,768]{1,0:T(8,128)(2,1)S(1)}, u32[]{:S(2)}, u32[]{:S(2)}) collective-permute-start(bf16[384,768]{1,0:T(8,128)(2,1)S(1)} %copy-done.5), channel_id=1, source_target_pairs={{0,3},{1,0},{2,1},{3,2},{4,7},{5,4},{6,5},{7,6},{8,11},{9,8},{10,9... | collective-permute-start | bytes 1769480 | tf_op jit(solution)/shard_map/ppermute | solution.py:46
  97.2 105.0 %all-to-all-start.1 = ((bf16[8,96,768]{2,1,0:T(8,128)(2,1)}), bf16[8,96,768]{2,1,0:T(8,128)(2,1)S(1)}, u32[]{:S(2)}, u32[]{:S(2)}) async-start(bf16[8,96,768]{2,1,0:T(8,128)(2,1)} %broadcast_in_dim.81), calls=%async_computation.1 | async-start | bytes 2359296 | tf_op jit(solution)/shard_map/all_to_all | solution.py:964
  100.8 284.1 %reduce-scatter.3.cloned.1.call-start = ((), (), s32[]{:S(2)}) async-start(), calls=%async_computation.10 | async-start | bytes 11943936 | tf_op jit(solution)/shard_map/reduce_scatter | solution.py:1062
  103.1 66.0 %collective-permute-start.8 = (bf16[384,768]{1,0:T(8,128)(2,1)S(1)}, bf16[384,768]{1,0:T(8,128)(2,1)}, u32[]{:S(2)}, u32[]{:S(2)}) collective-permute-start(bf16[384,768]{1,0:T(8,128)(2,1)S(1)} %copy-done.5), channel_id=1, source_target_pairs={{0,2},{1,3},{2,0},{3,1},{4,6},{5,7},{6,4},{7,5},{8,10},{9,11},{10,... | collective-permute-start | bytes 1769480 | tf_op jit(solution)/shard_map/ppermute | solution.py:46
  123.2 45.9 %copy-start.18 = (bf16[384,768]{1,0:T(8,128)(2,1)}, bf16[384,768]{1,0:T(8,128)(2,1)S(1)}, u32[]{:S(2)}) copy-start(bf16[384,768]{1,0:T(8,128)(2,1)S(1)} %collective-permute-done.3.refs_4_) | copy-start | bytes 1769476
  123.2 78.9 %collective-permute-start.5 = (bf16[192,1536]{1,0:T(8,128)(2,1)}, bf16[192,1536]{1,0:T(8,128)(2,1)}, u32[]{:S(2)}, u32[]{:S(2)}) collective-permute-start(bf16[192,1536]{1,0:T(8,128)(2,1)} %get-tuple-element.150.refs_5_), channel_id=1, source_target_pairs={{0,1},{1,2},{2,3},{3,0},{4,5},{5,6},{6,7},{7,4},{8,9},{9,10},{10,1... | collective-permute-start | bytes 1769480 | tf_op jit(solution)/shard_map/ppermute | solution.py:46
  123.9 78.3 %collective-permute-start.6 = (bf16[192,1536]{1,0:T(8,128)(2,1)}, bf16[192,1536]{1,0:T(8,128)(2,1)}, u32[]{:S(2)}, u32[]{:S(2)}) collective-permute-start(bf16[192,1536]{1,0:T(8,128)(2,1)} %get-tuple-element.150.refs_5_), channel_id=1, source_target_pairs={{0,2},{1,3},{2,0},{3,1},{4,6},{5,7},{6,4},{7,5},{8,10},{9,11},{10,... | collective-permute-start | bytes 1769480 | tf_op jit(solution)/shard_map/ppermute | solution.py:46
  126.3 75.9 %collective-permute-start.7 = (bf16[192,1536]{1,0:T(8,128)(2,1)}, bf16[192,1536]{1,0:T(8,128)(2,1)}, u32[]{:S(2)}, u32[]{:S(2)}) collective-permute-start(bf16[192,1536]{1,0:T(8,128)(2,1)} %get-tuple-element.150.refs_5_), channel_id=1, source_target_pairs={{0,3},{1,0},{2,1},{3,2},{4,7},{5,4},{6,5},{7,6},{8,11},{9,8},{10,9... | collective-permute-start | bytes 1769480 | tf_op jit(solution)/shard_map/ppermute | solution.py:46
  278.0 19.8 %collective-permute-start.10 = (bf16[384,768]{1,0:T(8,128)(2,1)S(1)}, bf16[384,768]{1,0:T(8,128)(2,1)S(1)}, u32[]{:S(2)}, u32[]{:S(2)}) collective-permute-start(bf16[384,768]{1,0:T(8,128)(2,1)S(1)} %get-tuple-element.259), channel_id=1, source_target_pairs={{0,1},{1,2},{2,3},{3,0},{4,5},{5,6},{6,7},{7,4},{8,9},{9,10},{10,1... | collective-permute-start | bytes 1769480 | tf_op jit(solution)/shard_map/ppermute | solution.py:66
  278.0 25.3 %collective-permute-start.9 = (bf16[384,768]{1,0:T(8,128)(2,1)S(1)}, bf16[384,768]{1,0:T(8,128)(2,1)S(1)}, u32[]{:S(2)}, u32[]{:S(2)}) collective-permute-start(bf16[384,768]{1,0:T(8,128)(2,1)S(1)} %get-tuple-element.260), channel_id=1, source_target_pairs={{0,3},{1,0},{2,1},{3,2},{4,7},{5,4},{6,5},{7,6},{8,11},{9,8},{10,9... | collective-permute-start | bytes 1769480 | tf_op jit(solution)/shard_map/ppermute | solution.py:66
  304.2 30.9 %collective-permute-start.11 = (bf16[384,768]{1,0:T(8,128)(2,1)S(1)}, bf16[384,768]{1,0:T(8,128)(2,1)S(1)}, u32[]{:S(2)}, u32[]{:S(2)}) collective-permute-start(bf16[384,768]{1,0:T(8,128)(2,1)S(1)} %get-tuple-element.258), channel_id=1, source_target_pairs={{0,2},{1,3},{2,0},{3,1},{4,6},{5,7},{6,4},{7,5},{8,10},{9,11},{10,... | collective-permute-start | bytes 1769480 | tf_op jit(solution)/shard_map/ppermute | solution.py:66
  343.0 38.3 %all-to-all-start.2 = ((bf16[4,192,384]{2,1,0:T(8,128)(2,1)}), bf16[4,192,384]{2,1,0:T(8,128)(2,1)S(1)}, u32[]{:S(2)}, u32[]{:S(2)}) async-start(bf16[4,192,384]{2,1,0:T(8,128)(2,1)} %get-tuple-element.173), calls=%async_computation.2 | async-start | bytes 1179648 | tf_op jit(solution)/shard_map/all_to_all | solution.py:1066
  346.5 145.1 %reduce-scatter.5.cloned.1.call-start = ((), (), s32[]{:S(2)}) async-start(), calls=%async_computation.11 | async-start | bytes 11943936 | tf_op jit(solution)/shard_map/reduce_scatter | solution.py:1077
  348.0 22.4 %collective-permute-start.12 = (bf16[384,768]{1,0:T(8,128)(2,1)}, bf16[384,768]{1,0:T(8,128)(2,1)S(1)}, u32[]{:S(2)}, u32[]{:S(2)}) collective-permute-start(bf16[384,768]{1,0:T(8,128)(2,1)} %get-tuple-element.257), channel_id=1, source_target_pairs={{0,3},{1,0},{2,1},{3,2},{4,7},{5,4},{6,5},{7,6},{8,11},{9,8},{10,9... | collective-permute-start | bytes 1769480 | tf_op jit(solution)/shard_map/ppermute | solution.py:66
  351.8 29.5 %collective-permute-start.13 = (bf16[384,768]{1,0:T(8,128)(2,1)}, bf16[384,768]{1,0:T(8,128)(2,1)}, u32[]{:S(2)}, u32[]{:S(2)}) collective-permute-start(bf16[384,768]{1,0:T(8,128)(2,1)} %get-tuple-element.256), channel_id=1, source_target_pairs={{0,1},{1,2},{2,3},{3,0},{4,5},{5,6},{6,7},{7,4},{8,9},{9,10},{10,1... | collective-permute-start | bytes 1769480 | tf_op jit(solution)/shard_map/ppermute | solution.py:66
  387.6 33.6 %all-to-all-start.3 = ((bf16[8,96,768]{2,1,0:T(8,128)(2,1)}), bf16[8,96,768]{2,1,0:T(8,128)(2,1)}, u32[]{:S(2)}, u32[]{:S(2)}) async-start(bf16[8,96,768]{2,1,0:T(8,128)(2,1)} %bitcast.20), calls=%async_computation.4 | async-start | bytes 2359296 | tf_op jit(solution)/shard_map/all_to_all | solution.py:957
  391.9 30.7 %collective-permute-start.14 = (bf16[384,768]{1,0:T(8,128)(2,1)S(1)}, bf16[384,768]{1,0:T(8,128)(2,1)}, u32[]{:S(2)}, u32[]{:S(2)}) collective-permute-start(bf16[384,768]{1,0:T(8,128)(2,1)S(1)} %copy-done.16), channel_id=1, source_target_pairs={{0,2},{1,3},{2,0},{3,1},{4,6},{5,7},{6,4},{7,5},{8,10},{9,11},{10,... | collective-permute-start | bytes 1769480 | tf_op jit(solution)/shard_map/ppermute | solution.py:66
  434.2 17.1 %collective-permute-start.16 = (bf16[416,768]{1,0:T(8,128)(2,1)}, bf16[416,768]{1,0:T(8,128)(2,1)}, u32[]{:S(2)}, u32[]{:S(2)}) collective-permute-start(bf16[416,768]{1,0:T(8,128)(2,1)} %get-tuple-element.252), channel_id=1, source_target_pairs={{0,3},{1,0},{2,1},{3,2},{4,7},{5,4},{6,5},{7,6},{8,11},{9,8},{10,9... | collective-permute-start | bytes 1916936 | tf_op jit(solution)/shard_map/ppermute | solution.py:66
  436.1 29.6 %collective-permute-start.17 = (bf16[416,768]{1,0:T(8,128)(2,1)}, bf16[416,768]{1,0:T(8,128)(2,1)}, u32[]{:S(2)}, u32[]{:S(2)}) collective-permute-start(bf16[416,768]{1,0:T(8,128)(2,1)} %get-tuple-element.251), channel_id=1, source_target_pairs={{0,1},{1,2},{2,3},{3,0},{4,5},{5,6},{6,7},{7,4},{8,9},{9,10},{10,1... | collective-permute-start | bytes 1916936 | tf_op jit(solution)/shard_map/ppermute | solution.py:66
  447.8 43.9 %collective-permute-start.15 = (bf16[416,768]{1,0:T(8,128)(2,1)}, bf16[416,768]{1,0:T(8,128)(2,1)}, u32[]{:S(2)}, u32[]{:S(2)}) collective-permute-start(bf16[416,768]{1,0:T(8,128)(2,1)} %get-tuple-element.253), channel_id=1, source_target_pairs={{0,2},{1,3},{2,0},{3,1},{4,6},{5,7},{6,4},{7,5},{8,10},{9,11},{10,... | collective-permute-start | bytes 1916936 | tf_op jit(solution)/shard_map/ppermute | solution.py:66
  467.0 19.0 %all-to-all-start.4 = ((bf16[8,96,576]{2,1,0:T(8,128)(2,1)}), bf16[8,96,576]{2,1,0:T(8,128)(2,1)}, u32[]{:S(2)}, u32[]{:S(2)}) async-start(bf16[8,96,576]{2,1,0:T(8,128)(2,1)} %bitcast.94), calls=%async_computation.5 | async-start | bytes 1966080 | tf_op jit(solution)/shard_map/all_to_all | solution.py:957
  500.9 24.3 %all-to-all-start.5 = ((f32[32,1,624]{2,1,0:T(1,128)}), f32[32,1,624]{2,1,0:T(1,128)S(1)}, u32[]{:S(2)}, u32[]{:S(2)}) async-start(f32[32,1,624]{2,1,0:T(1,128)} %copy.201), calls=%async_computation.7 | async-start | bytes 163840 | tf_op jit(solution)/shard_map/all_to_all | solution.py:1133
  (42 other events, 301.2 us)
Sparse Core Ops, SparseCore 0:
  10.5 71.0 all-gather.3
  86.9 74.1 all-gather.5
  303.5 81.3 reduce-scatter.2
  388.3 82.1 reduce-scatter.4
where the time goes:
time: 544 us; the launch traced here: 535 us
  Pallas kernels  243 us (45%)
  waiting for transfers between devices  90.8 us (17%)
  starting transfers between devices  65.4 us (12%)
  local copies, waits for them, and re-layouts  39 us (7%)
  other arithmetic  38.6 us (7%)
  blocking collectives  28 us (5%)
  between operations  15.2 us (3%)
  matrix products  15 us (3%)
    pallas_call x1, Pallas kernels, experts_main(): pl.pallas_call(functools.partial(experts_kernel, experts=experts), out_sh...  59.1 us
    ppermute x9, waiting for transfers between devices, ring_scatter(): lax.ppermute(parts[shift], 'mp', [(i, (i - shift) % width) for i in range...  37.3 us
    ppermute x9, waiting for transfers between devices, ring_gather(): lax.ppermute(block, 'mp', [(i, (i + shift) % width) for i in range(width)])  36 us
    pallas_call x2, Pallas kernels, slab_product(): pl.pallas_call(functools.partial(slab_kernel, experts=experts), out_shape...  32.2 us
    pallas_call x2, Pallas kernels, experts_before(): pl.pallas_call(functools.partial(before_kernel, count=count, shared=share...  28.1 us
    pallas_call x1, Pallas kernels, experts_out(): pl.pallas_call(functools.partial(branch_kernel, experts=experts), out_sha...  27.2 us
    pallas_call x1, Pallas kernels, attend_back(): pl.pallas_call(functools.partial(attend_back_kernel, group=group), out_sh...  25.2 us
    convert_element_type x7, other arithmetic, adamw_update(): return (master_new, first_new, second_new, master_new.astype(bf16))  21 us
  transfers between devices with their start and end apart: 28, of which 9 were waited for; matrix products, arithmetic and copies ran while one was open for 14% of the time, Pallas kernels for 33%

commit v1 on v0

--- a/solution.py
+++ b/solution.py
@@ -58,11 +58,9 @@
     return [terms[0]] + [found[i] for i in range(1, width)], near, far
 
 
-def ring_scatter(partial):
+def ring_scatter(parts):
     width = lax.axis_size("mp")
-    extent = partial.shape[0] // width
-    parts = [partial[i * extent : (i + 1) * extent] for i in range(width)]
-    return parts[:1] + [
+    return [parts[0]] + [
         lax.ppermute(parts[shift], "mp", [(i, (i - shift) % width) for i in range(width)])
         for shift in range(1, width)
     ]
@@ -329,25 +327,20 @@
 
 
 def norm_two_kernel(*refs, width_mp, items):
-    rank_ref, segment_ref, table_ref, rows_ref, turned_ref = refs[:5]
-    mixed_refs = refs[5:-6]
-    h_ref, x_mine_ref, attn_mine_ref, mixed_mine_ref, proj_ref, proj_scratch = refs[-6:]
+    rank_ref, segment_ref, table_ref, rows_ref, proj_ref = refs[:5]
+    mixed_refs = refs[5:-4]
+    h_ref, x_mine_ref, attn_mine_ref, mixed_mine_ref = refs[-4:]
     step = pl.program_id(0)
     rank = rank_ref[0]
     segment = segment_ref[...]
     width = rows_ref.shape[1]
     heads = mixed_refs[0].shape[0]
 
-    @pl.when(step == 0)
-    def _():
-        proj_scratch[...] = turned_ref[...].T
-        proj_ref[...] = proj_scratch[...]
-
     attn = jnp.zeros(rows_ref.shape, f32)
     for place in range(width_mp):
         here = slice(place * heads, (place + 1) * heads)
         mixed = mixed_refs[place][...]
-        attn += dot(mixed, proj_scratch[here, :], TN)
+        attn += dot(mixed, proj_ref[here, :], TN)
 
         @pl.when(step == rank)
         def _():
@@ -366,7 +359,7 @@
     h_ref[...] = (normed * (1.0 + scale) + shift).astype(bf16)
 
 
-def norm_two(arrays, patches, proj_t, table, segment):
+def norm_two(arrays, patches, proj, table, segment):
     width_mp, (heads, group) = len(arrays), arrays[0].shape
     rows, width, items = group // width_mp, patches.shape[1], table.shape[0]
     every = heads * width_mp
@@ -377,7 +370,6 @@
             jax.ShapeDtypeStruct((rows, width), f32),
             jax.ShapeDtypeStruct((rows, width), f32),
             jax.ShapeDtypeStruct((every, rows), bf16),
-            jax.ShapeDtypeStruct((every, width), bf16),
         ),
         grid_spec=pltpu.PrefetchScalarGridSpec(
             num_scalar_prefetch=1,
@@ -386,7 +378,7 @@
                 pl.BlockSpec((rows, 1), lambda i, rank: (i, 0)),
                 plain(*table.shape),
                 pl.BlockSpec((rows, width), lambda i, rank: (i, 0)),
-                plain(*proj_t.shape),
+                plain(*proj.shape),
             ]
             + [pl.BlockSpec((heads, rows), lambda i, rank: (0, i))] * len(arrays),
             out_specs=(
@@ -394,20 +386,22 @@
                 plain(rows, width),
                 plain(rows, width),
                 plain(every, rows),
-                plain(every, width),
             ),
-            scratch_shapes=[pltpu.VMEM((every, width), bf16)],
         ),
         compiler_params=pltpu.CompilerParams(vmem_limit_bytes=VMEM),
         cost_estimate=SMALL,
         name="norm_two",
-    )(lax.axis_index("mp").reshape(1), segment, table, patches, proj_t, *arrays)
-
-
-def product_kernel(rank_ref, a_ref, b_ref, part_ref, out_ref):
+    )(lax.axis_index("mp").reshape(1), segment, table, patches, proj, *arrays)
+
+
+def product_kernel(rank_ref, a_ref, b_ref, part_ref, *out_refs):
     rows = a_ref.shape[0]
-    out_ref[0:rows, :] = dot(a_ref[...], b_ref[...], NT).astype(bf16)
-    out_ref[rows:, :] = part_ref[0]
+    for place, out_ref in enumerate(out_refs):
+
+        @pl.when(pl.program_id(0) == place)
+        def _():
+            out_ref[0:rows, :] = dot(a_ref[...], b_ref[...], NT).astype(bf16)
+            out_ref[rows:, :] = part_ref[0]
 
 
 def ring_product(a, b, parts):
@@ -415,7 +409,7 @@
     rows = a.shape[0] // width_mp
     return pl.pallas_call(
         product_kernel,
-        out_shape=jax.ShapeDtypeStruct((a.shape[0] + width_mp * extra, width), bf16),
+        out_shape=(jax.ShapeDtypeStruct((rows + extra, width), bf16),) * width_mp,
         grid_spec=pltpu.PrefetchScalarGridSpec(
             num_scalar_prefetch=1,
             grid=(width_mp,),
@@ -424,7 +418,7 @@
                 plain(*b.shape),
                 pl.BlockSpec((1, extra, width), lambda i, rank: (i, 0, 0)),
             ],
-            out_specs=pl.BlockSpec((rows + extra, width), lambda i, rank: (i, 0)),
+            out_specs=(plain(rows + extra, width),) * width_mp,
         ),
         compiler_params=pltpu.CompilerParams(vmem_limit_bytes=VMEM),
         cost_estimate=SMALL,
@@ -625,38 +619,25 @@
     return ((index == picked[:, 0:1]) | (index == picked[:, 1:2])).astype(bf16)
 
 
-def experts_kernel(
-    rank_ref,
-    place_ref,
-    places_ref,
-    picked_ref,
-    rows_ref,
-    weight_ref,
-    router_ref,
-    router_wide_ref,
-    slots_ref,
-    named_ref,
-    back_ref,
-    shared_back_ref,
-    dispatched_ref,
-    act_ref,
-    grad_pre_ref,
-    grad_res_ref,
-    gate_ref,
-    shared_act_ref,
-    shared_grad_ref,
-    grad_logits_ref,
-    grad_rows_ref,
-    grad_gates_ref,
-    grad_slots_ref,
-    high_ref,
-    rest_ref,
-    *,
-    experts,
-):
+def ring_store(out_refs, rank, owner, block):
+    width_mp = len(out_refs)
+    for place, out_ref in enumerate(out_refs):
+
+        @pl.when(lax.rem(rank - owner + width_mp, width_mp) == place)
+        def _():
+            out_ref[...] = block
+
+
+def experts_kernel(*refs, experts):
+    rank_ref, place_ref, places_ref, picked_ref, rows_ref, weight_ref = refs[:6]
+    router_ref, router_wide_ref, named_ref, back_ref, shared_back_ref = refs[6:11]
+    dispatched_ref, act_ref, grad_pre_ref, gate_ref = refs[11:15]
+    shared_act_ref, shared_grad_ref, grad_logits_ref = refs[15:18]
+    grad_rows_refs = refs[18:-4]
+    grad_gates_ref, grad_slots_ref, high_ref, rest_ref = refs[-4:]
     step = pl.program_id(0)
     group = rows_ref.shape[0]
-    capacity = slots_ref.shape[1]
+    capacity = back_ref.shape[1]
 
     @pl.when(step < experts)
     def _():
@@ -679,7 +660,6 @@
         back = back_ref[0].astype(f32)
         grad_pre = (gate * back * slope).astype(bf16)
         grad_pre_ref[0] = grad_pre
-        grad_res_ref[0] = (gate * slots_ref[0].astype(f32)).astype(bf16)
         grad_gate = jnp.sum(back * act.astype(f32), axis=1, keepdims=True)
         grad_gates_ref[step] = jnp.sum(jnp.where(picks, grad_gate, 0.0), axis=0, keepdims=True)
         here = pl.ds(pl.multiple_of(step * capacity, capacity), capacity)
@@ -711,40 +691,31 @@
         total += dot(grad_pre, weight_ref[0], NT)
         total += dot(high_ref[:, here], router_ref[...], TN)
         total += dot(rest_ref[:, here], router_ref[...], TN)
-        grad_rows_ref[...] = total.astype(bf16)
+        ring_store(grad_rows_refs, rank_ref[0], step - experts, total.astype(bf16))
 
 
 def row_block(experts, *shape):
     return pl.BlockSpec(shape, lambda e, *_: (jnp.maximum(e - experts, 0), 0))
 
 
-def ring_block(experts, width_mp, *shape):
-    def index(e, rank):
-        return (lax.rem(rank[0] - jnp.maximum(e - experts, 0) + width_mp, width_mp), 0)
-
-    return pl.BlockSpec(shape, index)
-
-
-def experts_main(places, picked, h_two, in_w, router, slots, named, back, shared_back):
+def experts_main(places, picked, h_two, in_w, router, named, back, shared_back):
     group, width = h_two.shape
     experts, capacity, hidden = back.shape
     width_mp = lax.axis_size("mp")
     rows = group // width_mp
-    slot_shape = jax.ShapeDtypeStruct((experts, capacity, width), bf16)
     unit_shape = jax.ShapeDtypeStruct((experts, capacity, hidden), bf16)
     return pl.pallas_call(
         functools.partial(experts_kernel, experts=experts),
         out_shape=(
-            slot_shape,
+            jax.ShapeDtypeStruct((experts, capacity, width), bf16),
             unit_shape,
             unit_shape,
-            slot_shape,
             jax.ShapeDtypeStruct((experts, capacity, 1), f32),
             jax.ShapeDtypeStruct((group, hidden), bf16),
             jax.ShapeDtypeStruct((group, hidden), bf16),
             jax.ShapeDtypeStruct((experts, group), f32),
-            jax.ShapeDtypeStruct((group, width), bf16),
-        ),
+        )
+        + (jax.ShapeDtypeStruct((rows, width), bf16),) * width_mp,
         grid_spec=pltpu.PrefetchScalarGridSpec(
             num_scalar_prefetch=1,
             grid=(experts + width_mp,),
@@ -756,7 +727,6 @@
                 per_slab(experts, width, hidden),
                 whole(experts, width),
                 whole(width, LANES),
-                per_expert(experts, capacity, width),
                 per_expert(experts, capacity, LANES),
                 per_expert(experts, capacity, hidden),
                 row_block(experts, rows, hidden),
@@ -765,13 +735,12 @@
                 per_expert(experts, capacity, width),
                 per_expert(experts, capacity, hidden),
                 per_expert(experts, capacity, hidden),
-                per_expert(experts, capacity, width),
                 per_expert(experts, capacity, 1),
                 row_block(experts, rows, hidden),
                 row_block(experts, rows, hidden),
                 whole(experts, group),
-                ring_block(experts, width_mp, rows, width),
-            ),
+            )
+            + (whole(rows, width),) * width_mp,
             scratch_shapes=[
                 pltpu.VMEM((experts, 1, group), f32),
                 pltpu.VMEM((experts * capacity, width), bf16),
@@ -791,29 +760,33 @@
         in_w,
         router.T,
         jnp.pad(router, ((0, 0), (0, LANES - experts))),
-        slots,
         named,
         back,
         shared_back,
     )
 
 
-def slab_kernel(a_ref, b_ref, a_shared_ref, b_shared_ref, out_ref, *, experts):
+def slab_kernel(a_ref, b_ref, a_shared_ref, b_shared_ref, *refs, experts):
     step = pl.program_id(0)
+    out_ref = refs[-1]
 
     @pl.when(step < experts)
     def _():
-        out_ref[0] = dot(a_ref[0], b_ref[0], TN).astype(bf16)
+        a = a_ref[0]
+        if len(refs) > 1:
+            a = (refs[0][0] * a.astype(f32)).astype(bf16)
+        out_ref[0] = dot(a, b_ref[0], TN).astype(bf16)
 
     @pl.when(step == experts)
     def _():
         out_ref[0] = dot(a_shared_ref[...], b_shared_ref[...], TN).astype(bf16)
 
 
-def slab_product(a, b, a_shared, b_shared, name):
+def slab_product(a, b, a_shared, b_shared, name, gates=None):
     experts, capacity, width = a.shape
     hidden = b.shape[2]
     group = a_shared.shape[0]
+    scaled = gates is not None
     return pl.pallas_call(
         functools.partial(slab_kernel, experts=experts),
         out_shape=jax.ShapeDtypeStruct((experts + 1, width, hidden), bf16),
@@ -823,17 +796,19 @@
             per_expert(experts, capacity, hidden),
             whole(group, width),
             whole(group, hidden),
-        ],
+        ]
+        + [per_expert(experts, capacity, 1)] * scaled,
         out_specs=per_slab(experts, width, hidden),
         compiler_params=pltpu.CompilerParams(vmem_limit_bytes=VMEM),
         cost_estimate=SMALL,
         name=name,
-    )(a, b, a_shared, b_shared)
+    )(a, b, a_shared, b_shared, *((gates,) * scaled))
 
 
 def branch_kernel(
-    rank_ref, picked_ref, gate_ref, act_ref, weight_ref, shared_ref, out_ref, res_ref, *, experts
+    rank_ref, picked_ref, gate_ref, act_ref, weight_ref, shared_ref, *refs, experts
 ):
+    out_refs, res_ref = refs[:-1], refs[-1]
     step = pl.program_id(0)
     capacity = act_ref.shape[1]
 
@@ -845,7 +820,8 @@
     @pl.when(step >= experts)
     def _():
         total = dot(slots_of(picked_ref[...], experts * capacity), res_ref[...])
-        out_ref[...] = (total + dot(shared_ref[...], weight_ref[0], NT)).astype(bf16)
+        total += dot(shared_ref[...], weight_ref[0], NT)
+        ring_store(out_refs, rank_ref[0], step - experts, total.astype(bf16))
 
 
 def experts_out(picked, gates, act, out_t, shared_act):
@@ -854,7 +830,7 @@
     rows = group // width_mp
     return pl.pallas_call(
         functools.partial(branch_kernel, experts=experts),
-        out_shape=jax.ShapeDtypeStruct((group, width), bf16),
+        out_shape=(jax.ShapeDtypeStruct((rows, width), bf16),) * width_mp,
         grid_spec=pltpu.PrefetchScalarGridSpec(
             num_scalar_prefetch=1,
             grid=(experts + width_mp,),
@@ -865,7 +841,7 @@
                 per_slab(experts, width, hidden),
                 row_block(experts, rows, hidden),
             ],
-            out_specs=ring_block(experts, width_mp, rows, width),
+            out_specs=(whole(rows, width),) * width_mp,
             scratch_shapes=[pltpu.VMEM((experts * capacity, width), bf16)],
         ),
         compiler_params=pltpu.CompilerParams(vmem_limit_bytes=VMEM),
@@ -1014,6 +990,8 @@
     cot_near = dict(zip(near, cot_near))
     cot_blocks = [cot_near.get(i, block) for i, block in enumerate(cot_blocks)]
     mixed_blocks = ring_gather(mixed_here)
+    proj = after(proj_t, mixed_here).T
+    proj, cot_blocks = lax.optimization_barrier((proj, cot_blocks))
     (grad_branch,) = by_rows(
         gated_kernel,
         1,
@@ -1025,29 +1003,27 @@
     )
     held = experts_before(place_of, names_low, grad_branch, out_t, capacity, E // 2)
     held = experts_before(place_of, names_low, grad_branch, out_t, capacity, E // 2, held)
-    mixed_blocks, held, proj_t = lax.optimization_barrier((mixed_blocks, held, proj_t))
+    mixed_blocks, held = lax.optimization_barrier((mixed_blocks, held))
     branch_slots, named_slots, back_slots, back_shared = held
-    h_two, x_one_mine, attn_mine, mixed_mine, proj = norm_two(
-        mixed_blocks, patches_all, proj_t, modulation, segment_column
+    h_two, x_one_mine, attn_mine, mixed_mine = norm_two(
+        mixed_blocks, patches_all, proj, modulation, segment_column
     )
 
     (
         dispatched,
         expert_act,
         grad_expert_pre,
-        grad_res,
         gates,
         shared_act,
         grad_shared_pre,
         grad_logits,
-        grad_h_two,
+        *grad_h_two,
     ) = experts_main(
         place_of,
         picked,
         h_two,
         in_w,
         router_matrix,
-        branch_slots,
         named_slots,
         back_slots,
         back_shared,
@@ -1056,7 +1032,7 @@
 
     two_terms, grad_out_slab, mlp_part = sent_beside(
         two_terms,
-        slab_product(grad_res, expert_act, grad_branch, shared_act, "grad_out"),
+        slab_product(branch_slots, expert_act, grad_branch, shared_act, "grad_out", gates),
         lambda near: experts_out(picked, after(gates, near), expert_act, out_t, shared_act),
     )
     grad_out_mine = lax.psum_scatter(grad_out_slab, "dp", scatter_dimension=1, tiled=True)

time: 544 us -> 535 us (0.983)
  local copies, waits for them, and re-layouts: 39 us -> 29.7 us
  waiting for transfers between devices: 90.8 us -> 98.3 us
  Pallas kernels: 243 us -> 236 us
    slice x3 -> x0, local copies, waits for them, and re-layouts: 7.32 us -> none  [ring_scatter(): parts = [partial[i * extent:(i + 1) * extent] for i in range(width)]]
    ppermute x9, waiting for transfers between devices: 37.3 us -> 44.2 us  [ring_scatter(): lax.ppermute(parts[shift], 'mp', [(i, (i - shift) % width) for i in range...]
  transfers between devices with their start and end apart: 28 -> 28, of which waited for: 9 -> 11; matrix products, arithmetic and copies ran while one was open for 14% -> 13% of each run, Pallas kernels for 33% -> 33%
where the time goes in v1:
time: 535 us; the launch traced here: 525 us
  Pallas kernels  236 us (44%)
  waiting for transfers between devices  98.3 us (18%)
  starting transfers between devices  65.7 us (12%)
  other arithmetic  37.6 us (7%)
  local copies, waits for them, and re-layouts  29.7 us (6%)
  blocking collectives  28 us (5%)
  matrix products  14.9 us (3%)
  between operations  14.8 us (3%)
    pallas_call x1, Pallas kernels, experts_main(): pl.pallas_call(functools.partial(experts_kernel, experts=experts), out_sh...  57.5 us
    ppermute x9, waiting for transfers between devices, ring_scatter(): lax.ppermute(parts[shift], 'mp', [(i, (i - shift) % width) for i in range...  44.2 us
    ppermute x9, waiting for transfers between devices, ring_gather(): lax.ppermute(block, 'mp', [(i, (i + shift) % width) for i in range(width)])  37.6 us
    pallas_call x2, Pallas kernels, slab_product(): pl.pallas_call(functools.partial(slab_kernel, experts=experts), out_shape...  33.3 us
    pallas_call x2, Pallas kernels, experts_before(): pl.pallas_call(functools.partial(before_kernel, count=count, shared=share...  28.1 us
    pallas_call x1, Pallas kernels, experts_out(): pl.pallas_call(functools.partial(branch_kernel, experts=experts), out_sha...  27.9 us
    pallas_call x1, Pallas kernels, attend_back(): pl.pallas_call(functools.partial(attend_back_kernel, group=group), out_sh...  21.5 us
    convert_element_type x7, other arithmetic, adamw_update(): return (master_new, first_new, second_new, master_new.astype(bf16))  21.1 us
  transfers between devices with their start and end apart: 28, of which 11 were waited for; matrix products, arithmetic and copies ran while one was open for 13% of the time, Pallas kernels for 33%

profile of v1, /device:TPU:0, one launch (start us, length us, event | category | flops | bytes accessed | tf_op | source)
XLA Modules:
  0.0 525.2 jit_solution(12474534024960067919)
XLA Ops:
  17.8 10.1 %all-gather = bf16[8,3,768]{2,1,0:T(4,128)(2,1)} all-gather(bf16[1,3,768]{2,1,0:T(4,128)(2,1)S(1)} %bitcast.109), channel_id=1, replica_groups=mesh['dp'=8,'mp'=4] {'dp'}, dimensions={0}, use_global_device_ids=true | all-gather | bytes 41472 | tf_op jit(solution)/shard_map/all_gather | solution.py:942
  41.2 17.9 %all_gather.13.refs_4_ = bf16[768,576]{1,0:T(8,128)(2,1)} all-gather(bf16[96,576]{1,0:T(8,128)(2,1)} %convert_element_type.122), channel_id=1, replica_groups=mesh['dp'=8,'mp'=4] {'dp'}, dimensions={0}, use_global_device_ids=true | all-gather | bytes 995328 | tf_op jit(solution)/shard_map/all_gather | solution.py:951
  61.7 12.9 %all-to-all-done = f32[32,1,624]{2,1,0:T(1,128)} async-done(((f32[32,1,624]{2,1,0:T(1,128)}), f32[32,1,624]{2,1,0:T(1,128)}, u32[]{:S(2)}, u32[]{:S(2)}) %all-to-all-start) | async-done | bytes 79904 | tf_op jit(solution)/shard_map/all_to_all | solution.py:950
  76.5 10.2 %norm_one.1 = (bf16[1536,768]{1,0:T(8,128)(2,1)}, bf16[1536,768]{1,0:T(8,128)(2,1)}, bf16[1536,1152]{1,0:T(8,128)(2,1)}, bf16[768,1152]{1,0:T(8,128)(2,1)}) custom-call(s32[1]{0:T(128)} %bitcast.refs_0_.rank_ref, s32[1536,1]{1,0:T(8,128)} %broadcast_in_dim.83.refs_1_, f32[3,4608]{1,0:T(4,128)} %reshape.220.refs_2_.table_ref, ...), custom_call_target="tpu_custom_call" | custom-call | flops 1000000 | bytes 100000 | tf_op jit(solution)/shard_map/norm_one/pallas_call | solution.py:271
  97.2 3.6 all-to-all-start.1
  103.1 17.1 %attend.1 = (bf16[192,1536]{1,0:T(8,128)(2,1)}, f32[3,1,1536]{2,1,0:T(1,128)}) custom-call(s32[6]{0:T(128)} %subtract_minimum_fusion.start_ref, s32[6]{0:T(128)} %copy-done.40, bf16[1536,1152]{1,0:T(8,128)(2,1)} %get-tuple-element.145.qkv_ref), custom_call_target="tpu_custom_call" | custom-call | flops 1000000 | bytes 100000 | tf_op jit(solution)/shard_map/attend/pallas_call | solution.py:123
  131.5 37.6 %collective-permute-done.5.refs_5_ = bf16[384,768]{1,0:T(8,128)(2,1)} collective-permute-done((bf16[384,768]{1,0:T(8,128)(2,1)S(1)}, bf16[384,768]{1,0:T(8,128)(2,1)}, u32[]{:S(2)}, u32[]{:S(2)}) %collective-permute-start.5) | collective-permute-done | bytes 589856 | tf_op jit(solution)/shard_map/ppermute | solution.py:46
  169.1 5.0 grad_branch.1.branch_ref.a_shared_ref
  174.1 12.6 %experts_before.2 = (bf16[8,480,768]{2,1,0:T(8,128)(2,1)}, bf16[8,480,128]{2,1,0:T(8,128)(2,1)}, bf16[8,480,768]{2,1,0:T(8,128)(2,1)}) custom-call(s32[8,1,1536]{2,1,0:T(1,128)} %copy.195.place_ref.refs_1_, bf16[1536,128]{1,0:T(8,128)(2,1)} %pad_convert_fusion.named_ref, bf16[1536,768]{1,0:T(8,128)(2,1)} %grad_branch.1.branch_ref.a_shared_ref, ...), custom_call_target="tpu_custom_call" | custom-call | flops 1000000 | bytes 100000 | tf_op jit(solution)/shard_map/experts_before/pallas_call | solution.py:597
  186.7 15.5 %experts_before.3 = (bf16[8,480,768]{2,1,0:T(8,128)(2,1)}, bf16[8,480,128]{2,1,0:T(8,128)(2,1)}, bf16[8,480,768]{2,1,0:T(8,128)(2,1)}, bf16[1536,768]{1,0:T(8,128)(2,1)}) custom-call(s32[8,1,1536]{2,1,0:T(1,128)} %copy.195.place_ref.refs_1_, bf16[1536,128]{1,0:T(8,128)(2,1)} %pad_convert_fusion.named_ref, ...), custom_call_target="tpu_custom_call", output_to_operand_aliasing={{0}: (4, {}), {1}: (5, {}), {2}: (6, {})} | custom-call | flops 1000000 | bytes 100000 | tf_op jit(solution)/shard_map/experts_before/pallas_call | solution.py:597
  202.2 12.4 %norm_two.1 = (bf16[1536,768]{1,0:T(8,128)(2,1)}, f32[384,768]{1,0:T(8,128)}, f32[384,768]{1,0:T(8,128)}, bf16[768,384]{1,0:T(8,128)(2,1)}) custom-call(s32[1]{0:T(128)} %bitcast.refs_0_.rank_ref, s32[1536,1]{1,0:T(8,128)} %broadcast_in_dim.83.refs_1_, f32[3,4608]{1,0:T(4,128)} %reshape.220.refs_2_.table_ref, bf16[1536,768]{1,0:T(8,128)(2,1)} %get-tuple-element.146.refs_3_, ...), custom_call_target="tpu_custom_call" | custom-call | flops 1000000 | bytes 100000 | tf_op jit(solution)/shard_map/norm_two/pallas_call | solution.py:366
  214.6 57.5 %experts_main.1 = (bf16[8,480,768]{2,1,0:T(8,128)(2,1)}, bf16[8,480,768]{2,1,0:T(8,128)(2,1)}, bf16[8,480,768]{2,1,0:T(8,128)(2,1)}, f32[8,480,1]{2,1,0:T(8,128)...) custom-call(s32[1]{0:T(128)} %bitcast.refs_0_.rank_ref, ...), custom_call_target="tpu_custom_call" | custom-call | flops 1000000 | bytes 100000 | tf_op jit(solution)/shard_map/experts_main/pallas_call | solution.py:707
  272.2 3.8 collective-permute-start.9
  276.0 17.1 %grad_out.1 = bf16[9,768,768]{2,1,0:T(8,128)(2,1)} custom-call(bf16[8,480,768]{2,1,0:T(8,128)(2,1)} %get-tuple-element.184.a_ref, bf16[8,480,768]{2,1,0:T(8,128)(2,1)} %get-tuple-element.185.b_ref.act_ref, bf16[1536,768]{1,0:T(8,128)(2,1)} %grad_branch.1.branch_ref.a_shared_ref, bf16[1536,768]{1,0:T(8,128)(2,1)} %get-tuple-element.186.b_shared_ref.shared_ref, ...), custom_call_target="tpu_custom_call" | custom-call | flops 1000000 | bytes 100000 | tf_op jit(solution)/shard_map/grad_out/pallas_call | solution.py:790
  293.2 4.6 collective-permute-done.9.refs_1_
  302.0 27.9 %experts_out.1 = (bf16[384,768]{1,0:T(8,128)(2,1)}, bf16[384,768]{1,0:T(8,128)(2,1)}, bf16[384,768]{1,0:T(8,128)(2,1)}, bf16[384,768]{1,0:T(8,128)(2,1)}) custom-call(s32[1]{0:T(128)} %bitcast.refs_0_.rank_ref, s32[1536,2]{1,0:T(8,128)} %copy.196.refs_3_.picked_ref, f32[8,480,1]{2,1,0:T(8,128)} %get-tuple-element.191.refs_0_.gate_ref, ...), custom_call_target="tpu_custom_call" | custom-call | flops 1000000 | bytes 100000 | tf_op jit(solution)/shard_map/experts_out/pallas_call | solution.py:831
  330.8 6.8 %back_two.1 = (f32[384,768]{1,0:T(8,128)}, bf16[384,768]{1,0:T(8,128)(2,1)}, bf16[4,192,384]{2,1,0:T(8,128)(2,1)}, f32[3,2304]{1,0:T(4,128)}) custom-call(s32[1]{0:T(128)} %bitcast.refs_0_.rank_ref, s32[384,1]{1,0:T(8,128)} %dynamic_slice.4.segment_ref, f32[3,4608]{1,0:T(4,128)} %reshape.220.refs_2_.table_ref, bf16[384,768]{1,0:T(8,128)(2,1)} %get-tuple-element.181.refs_0_, ...), custom_call_target="tpu_custom_call" | custom-call | flops 1000000 | bytes 100000 | tf_op jit(solution)/shard_map/back_two/pallas_call | solution.py:465
  341.1 3.7 collective-permute-start.12
  344.8 16.2 %grad_in.1 = bf16[9,768,768]{2,1,0:T(8,128)(2,1)} custom-call(bf16[8,480,768]{2,1,0:T(8,128)(2,1)} %get-tuple-element.204.a_ref, bf16[8,480,768]{2,1,0:T(8,128)(2,1)} %get-tuple-element.205.b_ref, bf16[1536,768]{1,0:T(8,128)(2,1)} %get-tuple-element.176.refs_4_.a_shared_ref, bf16[1536,768]{1,0:T(8,128)(2,1)} %get-tuple-element.206.b_shared_ref), custom_call_target="tpu_custom_call" | custom-call | flops 1000000 | bytes 100000 | tf_op jit(solution)/shard_map/grad_in/pallas_call | solution.py:790
  365.0 11.2 %collective-permute-done.13.refs_2_ = bf16[384,768]{1,0:T(8,128)(2,1)} collective-permute-done((bf16[384,768]{1,0:T(8,128)(2,1)}, bf16[384,768]{1,0:T(8,128)(2,1)}, u32[]{:S(2)}, u32[]{:S(2)}) %collective-permute-start.13) | collective-permute-done | bytes 589856 | tf_op jit(solution)/shard_map/ppermute | solution.py:64
  389.5 21.5 %attend_back.1.a_ref = bf16[1536,1152]{1,0:T(8,128)(2,1)} custom-call(s32[6]{0:T(128)} %subtract_minimum_fusion.start_ref, s32[6]{0:T(128)} %copy-done.40, bf16[1536,1152]{1,0:T(8,128)(2,1)} %get-tuple-element.145.qkv_ref, bf16[192,1536]{1,0:T(8,128)(2,1)} %bitcast.99, f32[3,1,1536]{2,1,0:T(1,128)} %get-tuple-element.210.log_ref), custom_call_target="tpu_custom_call" | custom-call | flops 1000000 | bytes 100000 | tf_op jit(solution)/shard_map/attend_back/pallas_call | solution.py:185
  415.8 7.9 %grad_h_one.1 = (bf16[416,768]{1,0:T(8,128)(2,1)}, bf16[416,768]{1,0:T(8,128)(2,1)}, bf16[416,768]{1,0:T(8,128)(2,1)}, bf16[416,768]{1,0:T(8,128)(2,1)}) custom-call(s32[1]{0:T(128)} %bitcast.refs_0_.rank_ref, bf16[1536,1152]{1,0:T(8,128)(2,1)} %attend_back.1.a_ref, bf16[768,1152]{1,0:T(8,128)(2,1)} %get-tuple-element.216.b_ref, ...), custom_call_target="tpu_custom_call" | custom-call | flops 1000000 | bytes 100000 | tf_op jit(solution)/shard_map/grad_h_one/pallas_call | solution.py:410
  427.8 6.1 %convolution_convert_fusion = bf16[768,1152]{1,0:T(8,128)(2,1)} fusion(bf16[1536,768]{1,0:T(8,128)(2,1)} %get-tuple-element.225, bf16[1536,1152]{1,0:T(8,128)(2,1)S(1)} %copy-done.2), kind=kOutput, calls=%fused_computation.5 | convolution fusion | flops 2718793728 | bytes 7667712 | tf_op jit(solution)/shard_map/gd,gc->dc/dot_general | solution.py:1072
  436.7 5.4 %collective-permute-done.16.refs_1_ = bf16[416,768]{1,0:T(8,128)(2,1)} collective-permute-done((bf16[416,768]{1,0:T(8,128)(2,1)}, bf16[416,768]{1,0:T(8,128)(2,1)}, u32[]{:S(2)}, u32[]{:S(2)}) %collective-permute-start.16) | collective-permute-done | bytes 639008 | tf_op jit(solution)/shard_map/ppermute | solution.py:64
  442.1 14.2 %collective-permute-done.17.refs_3_ = bf16[416,768]{1,0:T(8,128)(2,1)} collective-permute-done((bf16[416,768]{1,0:T(8,128)(2,1)}, bf16[416,768]{1,0:T(8,128)(2,1)}, u32[]{:S(2)}, u32[]{:S(2)}) %collective-permute-start.17) | collective-permute-done | bytes 639008 | tf_op jit(solution)/shard_map/ppermute | solution.py:64
  457.6 4.2 all-to-all-start.4
  461.9 7.7 %fusion.26 = (bf16[8,768,96]{1,2,0:T(8,128)(2,1)}, f32[8,768,96]{1,2,0:T(8,128)}, f32[8,768,96]{1,2,0:T(8,128)}, f32[8,768,96]{1,2,0:T(8,128)}) fusion(f32[8,768,96]{1,2,0:T(8,128)} %param.57, f32[9,96,768]{2,1,0:T(8,128)S(1)} %copy-done.3, f32[8,768,96]{1,2,0:T(8,128)} %param.58, f32[8,768,96]{1,2,0:T(8,128)} %param.59), kind=kLoop, calls=%fused_computation.97 | loop fusion | flops 9437184 | bytes 17694720 | tf_op jit(solution)/shard_map/convert_element_type | solution.py:862
  472.1 3.7 outcome.1
  478.0 3.7 collective-permute-done.15.refs_2_
  484.3 4.7 back_one.1
  490.9 13.8 %all-to-all-start.5 = ((f32[32,1,624]{2,1,0:T(1,128)}), f32[32,1,624]{2,1,0:T(1,128)S(1)}, u32[]{:S(2)}, u32[]{:S(2)}) async-start(f32[32,1,624]{2,1,0:T(1,128)} %copy.207), calls=%async_computation.7 | async-start | bytes 163840 | tf_op jit(solution)/shard_map/all_to_all | solution.py:1109
  504.7 7.7 %fusion.28 = (bf16[8,96,768]{2,1,0:T(8,128)(2,1)}, f32[8,96,768]{2,1,0:T(8,128)}, f32[8,96,768]{2,1,0:T(8,128)}, f32[8,96,768]{2,1,0:T(8,128)}) fusion(f32[8,96,768]{2,1,0:T(8,128)} %param.54, f32[9,96,768]{2,1,0:T(8,128)S(1)} %convert_element_type.141, f32[8,96,768]{2,1,0:T(8,128)} %param.55, f32[8,96,768]{2,1,0:T(8,128)} %param.56), kind=kLoop, calls=%fused_computation.98 | loop fusion | flops 9437184 | bytes 17694720 | tf_op jit(solution)/shard_map/convert_element_type | solution.py:862
  (243 shorter events, 105.9 us)
Async XLA Ops:
  7.2 79.5 %all-gather.4.cloned.1.call-start = ((), (), s32[]{:S(2)}) async-start(), calls=%async_computation.8 | async-start | bytes 11943936 | tf_op jit(solution)/shard_map/all_gather | solution.py:919
  10.7 49.8 %copy-start.6 = (bf16[416,768]{1,0:T(8,128)(2,1)}, bf16[416,768]{1,0:T(8,128)(2,1)S(1)}, u32[]{:S(2)}) copy-start(bf16[416,768]{1,0:T(8,128)(2,1)S(1)} %fusion.5.refs_5_) | copy-start | bytes 1916932
  10.7 49.7 %copy-start.4 = (f32[8,96,768]{2,1,0:T(8,128)S(1)}, f32[8,96,768]{2,1,0:T(8,128)}, u32[]{:S(2)}) copy-start(f32[8,96,768]{2,1,0:T(8,128)} %param.54) | copy-start | bytes 7077892
  10.7 65.7 %collective-permute-start = (bf16[416,768]{1,0:T(8,128)(2,1)S(1)}, bf16[416,768]{1,0:T(8,128)(2,1)}, u32[]{:S(2)}, u32[]{:S(2)}) collective-permute-start(bf16[416,768]{1,0:T(8,128)(2,1)S(1)} %fusion.5.refs_5_), channel_id=1, source_target_pairs={{0,1},{1,2},{2,3},{3,0},{4,5},{5,6},{6,7},{7,4},{8,9},{9,10},{10,1... | collective-permute-start | bytes 1916936 | tf_op jit(solution)/shard_map/ppermute | solution.py:46
  13.8 62.7 %collective-permute-start.1 = (bf16[416,768]{1,0:T(8,128)(2,1)S(1)}, bf16[416,768]{1,0:T(8,128)(2,1)}, u32[]{:S(2)}, u32[]{:S(2)}) collective-permute-start(bf16[416,768]{1,0:T(8,128)(2,1)S(1)} %fusion.5.refs_5_), channel_id=1, source_target_pairs={{0,2},{1,3},{2,0},{3,1},{4,6},{5,7},{6,4},{7,5},{8,10},{9,11},{10,... | collective-permute-start | bytes 1916936 | tf_op jit(solution)/shard_map/ppermute | solution.py:46
  16.4 60.1 %collective-permute-start.2 = (bf16[416,768]{1,0:T(8,128)(2,1)S(1)}, bf16[416,768]{1,0:T(8,128)(2,1)}, u32[]{:S(2)}, u32[]{:S(2)}) collective-permute-start(bf16[416,768]{1,0:T(8,128)(2,1)S(1)} %fusion.5.refs_5_), channel_id=1, source_target_pairs={{0,3},{1,0},{2,1},{3,2},{4,7},{5,4},{6,5},{7,6},{8,11},{9,8},{10,9... | collective-permute-start | bytes 1916936 | tf_op jit(solution)/shard_map/ppermute | solution.py:46
  36.4 38.3 %all-to-all-start = ((f32[32,1,624]{2,1,0:T(1,128)}), f32[32,1,624]{2,1,0:T(1,128)}, u32[]{:S(2)}, u32[]{:S(2)}) async-start(f32[32,1,624]{2,1,0:T(1,128)} %all_to_all.28), calls=%async_computation | async-start | bytes 163840 | tf_op jit(solution)/shard_map/all_to_all | solution.py:950
  39.7 174.9 %all-gather.6.cloned.1.call-start = ((), (), s32[]{:S(2)}) async-start(), calls=%async_computation.9 | async-start | bytes 11943936 | tf_op jit(solution)/shard_map/all_gather | solution.py:984
  88.6 31.6 %collective-permute-start.3 = (bf16[384,768]{1,0:T(8,128)(2,1)S(1)}, bf16[384,768]{1,0:T(8,128)(2,1)S(1)}, u32[]{:S(2)}, u32[]{:S(2)}) collective-permute-start(bf16[384,768]{1,0:T(8,128)(2,1)S(1)} %copy-done.5), channel_id=1, source_target_pairs={{0,1},{1,2},{2,3},{3,0},{4,5},{5,6},{6,7},{7,4},{8,9},{9,10},{10,1... | collective-permute-start | bytes 1769480 | tf_op jit(solution)/shard_map/ppermute | solution.py:46
  89.6 30.6 %collective-permute-start.4 = (bf16[384,768]{1,0:T(8,128)(2,1)S(1)}, bf16[384,768]{1,0:T(8,128)(2,1)S(1)}, u32[]{:S(2)}, u32[]{:S(2)}) collective-permute-start(bf16[384,768]{1,0:T(8,128)(2,1)S(1)} %copy-done.5), channel_id=1, source_target_pairs={{0,3},{1,0},{2,1},{3,2},{4,7},{5,4},{6,5},{7,6},{8,11},{9,8},{10,9... | collective-permute-start | bytes 1769480 | tf_op jit(solution)/shard_map/ppermute | solution.py:46
  97.2 32.9 %all-to-all-start.1 = ((bf16[8,96,768]{2,1,0:T(8,128)(2,1)}), bf16[8,96,768]{2,1,0:T(8,128)(2,1)S(1)}, u32[]{:S(2)}, u32[]{:S(2)}) async-start(bf16[8,96,768]{2,1,0:T(8,128)(2,1)} %broadcast_in_dim.81), calls=%async_computation.1 | async-start | bytes 2359296 | tf_op jit(solution)/shard_map/all_to_all | solution.py:940
  100.8 278.2 %reduce-scatter.3.cloned.1.call-start = ((), (), s32[]{:S(2)}) async-start(), calls=%async_computation.10 | async-start | bytes 11943936 | tf_op jit(solution)/shard_map/reduce_scatter | solution.py:1038
  103.1 66.0 %collective-permute-start.5 = (bf16[384,768]{1,0:T(8,128)(2,1)S(1)}, bf16[384,768]{1,0:T(8,128)(2,1)}, u32[]{:S(2)}, u32[]{:S(2)}) collective-permute-start(bf16[384,768]{1,0:T(8,128)(2,1)S(1)} %copy-done.5), channel_id=1, source_target_pairs={{0,2},{1,3},{2,0},{3,1},{4,6},{5,7},{6,4},{7,5},{8,10},{9,11},{10,... | collective-permute-start | bytes 1769480 | tf_op jit(solution)/shard_map/ppermute | solution.py:46
  120.2 48.9 %copy-start.18 = (bf16[384,768]{1,0:T(8,128)(2,1)}, bf16[384,768]{1,0:T(8,128)(2,1)S(1)}, u32[]{:S(2)}) copy-start(bf16[384,768]{1,0:T(8,128)(2,1)S(1)} %collective-permute-done.3.refs_4_) | copy-start | bytes 1769476
  120.2 48.9 %copy-start.19 = (bf16[384,768]{1,0:T(8,128)(2,1)}, bf16[384,768]{1,0:T(8,128)(2,1)S(1)}, u32[]{:S(2)}) copy-start(bf16[384,768]{1,0:T(8,128)(2,1)S(1)} %collective-permute-done.4.refs_6_) | copy-start | bytes 1769476
  120.2 81.9 %collective-permute-start.6 = (bf16[192,1536]{1,0:T(8,128)(2,1)}, bf16[192,1536]{1,0:T(8,128)(2,1)}, u32[]{:S(2)}, u32[]{:S(2)}) collective-permute-start(bf16[192,1536]{1,0:T(8,128)(2,1)} %get-tuple-element.172.refs_5_), channel_id=1, source_target_pairs={{0,1},{1,2},{2,3},{3,0},{4,5},{5,6},{6,7},{7,4},{8,9},{9,10},{10,1... | collective-permute-start | bytes 1769480 | tf_op jit(solution)/shard_map/ppermute | solution.py:46
  120.9 81.3 %collective-permute-start.7 = (bf16[192,1536]{1,0:T(8,128)(2,1)}, bf16[192,1536]{1,0:T(8,128)(2,1)}, u32[]{:S(2)}, u32[]{:S(2)}) collective-permute-start(bf16[192,1536]{1,0:T(8,128)(2,1)} %get-tuple-element.172.refs_5_), channel_id=1, source_target_pairs={{0,2},{1,3},{2,0},{3,1},{4,6},{5,7},{6,4},{7,5},{8,10},{9,11},{10,... | collective-permute-start | bytes 1769480 | tf_op jit(solution)/shard_map/ppermute | solution.py:46
  123.2 78.9 %collective-permute-start.8 = (bf16[192,1536]{1,0:T(8,128)(2,1)}, bf16[192,1536]{1,0:T(8,128)(2,1)}, u32[]{:S(2)}, u32[]{:S(2)}) collective-permute-start(bf16[192,1536]{1,0:T(8,128)(2,1)} %get-tuple-element.172.refs_5_), channel_id=1, source_target_pairs={{0,3},{1,0},{2,1},{3,2},{4,7},{5,4},{6,5},{7,6},{8,11},{9,8},{10,9... | collective-permute-start | bytes 1769480 | tf_op jit(solution)/shard_map/ppermute | solution.py:46
  272.2 21.0 %collective-permute-start.10 = (bf16[384,768]{1,0:T(8,128)(2,1)}, bf16[384,768]{1,0:T(8,128)(2,1)S(1)}, u32[]{:S(2)}, u32[]{:S(2)}) collective-permute-start(bf16[384,768]{1,0:T(8,128)(2,1)} %get-tuple-element.183), channel_id=1, source_target_pairs={{0,1},{1,2},{2,3},{3,0},{4,5},{5,6},{6,7},{7,4},{8,9},{9,10},{10,1... | collective-permute-start | bytes 1769480 | tf_op jit(solution)/shard_map/ppermute | solution.py:64
  272.2 25.6 %collective-permute-start.9 = (bf16[384,768]{1,0:T(8,128)(2,1)}, bf16[384,768]{1,0:T(8,128)(2,1)S(1)}, u32[]{:S(2)}, u32[]{:S(2)}) collective-permute-start(bf16[384,768]{1,0:T(8,128)(2,1)} %get-tuple-element.182), channel_id=1, source_target_pairs={{0,3},{1,0},{2,1},{3,2},{4,7},{5,4},{6,5},{7,6},{8,11},{9,8},{10,9... | collective-permute-start | bytes 1769480 | tf_op jit(solution)/shard_map/ppermute | solution.py:64
  298.7 31.3 %collective-permute-start.11 = (bf16[384,768]{1,0:T(8,128)(2,1)S(1)}, bf16[384,768]{1,0:T(8,128)(2,1)S(1)}, u32[]{:S(2)}, u32[]{:S(2)}) collective-permute-start(bf16[384,768]{1,0:T(8,128)(2,1)S(1)} %copy-done.43), channel_id=1, source_target_pairs={{0,2},{1,3},{2,0},{3,1},{4,6},{5,7},{6,4},{7,5},{8,10},{9,11},{10,... | collective-permute-start | bytes 1769480 | tf_op jit(solution)/shard_map/ppermute | solution.py:64
  337.6 38.6 %all-to-all-start.2 = ((bf16[4,192,384]{2,1,0:T(8,128)(2,1)}), bf16[4,192,384]{2,1,0:T(8,128)(2,1)S(1)}, u32[]{:S(2)}, u32[]{:S(2)}) async-start(bf16[4,192,384]{2,1,0:T(8,128)(2,1)} %get-tuple-element.200), calls=%async_computation.2 | async-start | bytes 1179648 | tf_op jit(solution)/shard_map/all_to_all | solution.py:1042
  341.0 140.6 %reduce-scatter.5.cloned.1.call-start = ((), (), s32[]{:S(2)}) async-start(), calls=%async_computation.11 | async-start | bytes 11943936 | tf_op jit(solution)/shard_map/reduce_scatter | solution.py:1053
  341.1 23.9 %collective-permute-start.12 = (bf16[384,768]{1,0:T(8,128)(2,1)}, bf16[384,768]{1,0:T(8,128)(2,1)S(1)}, u32[]{:S(2)}, u32[]{:S(2)}) collective-permute-start(bf16[384,768]{1,0:T(8,128)(2,1)} %get-tuple-element.207), channel_id=1, source_target_pairs={{0,3},{1,0},{2,1},{3,2},{4,7},{5,4},{6,5},{7,6},{8,11},{9,8},{10,9... | collective-permute-start | bytes 1769480 | tf_op jit(solution)/shard_map/ppermute | solution.py:64
  344.8 31.3 %collective-permute-start.13 = (bf16[384,768]{1,0:T(8,128)(2,1)}, bf16[384,768]{1,0:T(8,128)(2,1)}, u32[]{:S(2)}, u32[]{:S(2)}) collective-permute-start(bf16[384,768]{1,0:T(8,128)(2,1)} %get-tuple-element.208), channel_id=1, source_target_pairs={{0,1},{1,2},{2,3},{3,0},{4,5},{5,6},{6,7},{7,4},{8,9},{9,10},{10,1... | collective-permute-start | bytes 1769480 | tf_op jit(solution)/shard_map/ppermute | solution.py:64
  381.7 29.3 %all-to-all-start.3 = ((bf16[8,96,768]{2,1,0:T(8,128)(2,1)}), bf16[8,96,768]{2,1,0:T(8,128)(2,1)S(1)}, u32[]{:S(2)}, u32[]{:S(2)}) async-start(bf16[8,96,768]{2,1,0:T(8,128)(2,1)} %bitcast.21), calls=%async_computation.4 | async-start | bytes 2359296 | tf_op jit(solution)/shard_map/all_to_all | solution.py:933
  385.3 29.4 %collective-permute-start.14 = (bf16[384,768]{1,0:T(8,128)(2,1)}, bf16[384,768]{1,0:T(8,128)(2,1)S(1)}, u32[]{:S(2)}, u32[]{:S(2)}) collective-permute-start(bf16[384,768]{1,0:T(8,128)(2,1)} %get-tuple-element.214), channel_id=1, source_target_pairs={{0,2},{1,3},{2,0},{3,1},{4,6},{5,7},{6,4},{7,5},{8,10},{9,11},{10,... | collective-permute-start | bytes 1769480 | tf_op jit(solution)/shard_map/ppermute | solution.py:64
  423.7 18.4 %collective-permute-start.16 = (bf16[416,768]{1,0:T(8,128)(2,1)}, bf16[416,768]{1,0:T(8,128)(2,1)}, u32[]{:S(2)}, u32[]{:S(2)}) collective-permute-start(bf16[416,768]{1,0:T(8,128)(2,1)} %get-tuple-element.223), channel_id=1, source_target_pairs={{0,3},{1,0},{2,1},{3,2},{4,7},{5,4},{6,5},{7,6},{8,11},{9,8},{10,9... | collective-permute-start | bytes 1916936 | tf_op jit(solution)/shard_map/ppermute | solution.py:64
  427.0 29.3 %collective-permute-start.17 = (bf16[416,768]{1,0:T(8,128)(2,1)}, bf16[416,768]{1,0:T(8,128)(2,1)}, u32[]{:S(2)}, u32[]{:S(2)}) collective-permute-start(bf16[416,768]{1,0:T(8,128)(2,1)} %get-tuple-element.224), channel_id=1, source_target_pairs={{0,1},{1,2},{2,3},{3,0},{4,5},{5,6},{6,7},{7,4},{8,9},{9,10},{10,1... | collective-permute-start | bytes 1916936 | tf_op jit(solution)/shard_map/ppermute | solution.py:64
  427.2 54.4 %collective-permute-start.15 = (bf16[416,768]{1,0:T(8,128)(2,1)}, bf16[416,768]{1,0:T(8,128)(2,1)}, u32[]{:S(2)}, u32[]{:S(2)}) collective-permute-start(bf16[416,768]{1,0:T(8,128)(2,1)} %get-tuple-element.218), channel_id=1, source_target_pairs={{0,2},{1,3},{2,0},{3,1},{4,6},{5,7},{6,4},{7,5},{8,10},{9,11},{10,... | collective-permute-start | bytes 1916936 | tf_op jit(solution)/shard_map/ppermute | solution.py:64
  457.6 19.0 %all-to-all-start.4 = ((bf16[8,96,576]{2,1,0:T(8,128)(2,1)}), bf16[8,96,576]{2,1,0:T(8,128)(2,1)}, u32[]{:S(2)}, u32[]{:S(2)}) async-start(bf16[8,96,576]{2,1,0:T(8,128)(2,1)} %bitcast.97), calls=%async_computation.5 | async-start | bytes 1966080 | tf_op jit(solution)/shard_map/all_to_all | solution.py:933
  490.9 24.9 %all-to-all-start.5 = ((f32[32,1,624]{2,1,0:T(1,128)}), f32[32,1,624]{2,1,0:T(1,128)S(1)}, u32[]{:S(2)}, u32[]{:S(2)}) async-start(f32[32,1,624]{2,1,0:T(1,128)} %copy.207), calls=%async_computation.7 | async-start | bytes 163840 | tf_op jit(solution)/shard_map/all_to_all | solution.py:1109
  (43 other events, 333.1 us)
Sparse Core Ops, SparseCore 0:
  10.5 71.0 all-gather.3
  86.9 74.1 all-gather.5
  298.0 80.9 reduce-scatter.2
  382.3 82.1 reduce-scatter.4

commit v2 on v1

--- a/solution.py
+++ b/solution.py
@@ -980,15 +980,15 @@
     proj_here = jnp.concatenate(
         [b[rows : rows + proj_rows].reshape(proj_shape) for b in patches_blocks], axis=1
     )
-    qkv, out_t = lax.optimization_barrier((qkv, out_t))
+    near, far = (1, width - 1), tuple(range(2, width - 1))
+    qkv, out_t, cot_near = lax.optimization_barrier((qkv, out_t, [cot_blocks[i] for i in near]))
     in_w = lax.all_gather(after(in_slab, out_t), "dp", axis=1, tiled=True)
     proj_t = from_dp(after(proj_here, qkv))
-    near, far = (1, width - 1), tuple(range(2, width - 1))
-    mixed_here, logs, cot_near = lax.optimization_barrier(
-        (*attend(qkv, start, kind), [cot_blocks[i] for i in near])
-    )
-    cot_near = dict(zip(near, cot_near))
-    cot_blocks = [cot_near.get(i, block) for i, block in enumerate(cot_blocks)]
+    mixed_here, logs, cot_far = lax.optimization_barrier(
+        (*attend(qkv, start, kind), [cot_blocks[i] for i in far])
+    )
+    arrived = dict(zip(near + far, cot_near + cot_far))
+    cot_blocks = [arrived.get(i, block) for i, block in enumerate(cot_blocks)]
     mixed_blocks = ring_gather(mixed_here)
     proj = after(proj_t, mixed_here).T
     proj, cot_blocks = lax.optimization_barrier((proj, cot_blocks))

time: 535 us -> 527 us (0.985)
  starting transfers between devices: 65.7 us -> 83.2 us
  waiting for transfers between devices: 98.3 us -> 81.9 us
  blocking collectives: 28 us -> 21 us
    ppermute x9, waiting for transfers between devices: 37.6 us -> 23.9 us  [ring_gather(): lax.ppermute(block, 'mp', [(i, (i + shift) % width) for i in range(width)])]
    all_to_all x2, waiting for transfers between devices: 12.9 us -> 0.01 us  [body(): received = lax.all_to_all(payload, ('dp', 'mp'), 0, 0, tiled=True)]
    ppermute x9, starting transfers between devices: 17 us -> 28.6 us  [ring_gather(): lax.ppermute(block, 'mp', [(i, (i + shift) % width) for i in range(width)])]
    ppermute x9, waiting for transfers between devices: 44.2 us -> 52.6 us  [ring_scatter(): lax.ppermute(parts[shift], 'mp', [(i, (i - shift) % width) for i in range...]
    ppermute x9, starting transfers between devices: 16.6 us -> 23.8 us  [ring_scatter(): lax.ppermute(parts[shift], 'mp', [(i, (i - shift) % width) for i in range...]
    all_gather x1, blocking collectives: 17.9 us -> 11.9 us  [body(): lax.all_gather(after(qkv_weight.astype(bf16), cond_all), 'dp', axis=0, ti...]
  transfers between devices with their start and end apart: 28 -> 28, of which waited for: 11 -> 11; matrix products, arithmetic and copies ran while one was open for 13% -> 13% of each run, Pallas kernels for 33% -> 34%
where the time goes in v2:
time: 527 us; the launch traced here: 517 us
  Pallas kernels  236 us (45%)
  starting transfers between devices  83.2 us (16%)
  waiting for transfers between devices  81.9 us (16%)
  other arithmetic  36.9 us (7%)
  local copies, waits for them, and re-layouts  28.4 us (5%)
  blocking collectives  21 us (4%)
  between operations  14.8 us (3%)
  matrix products  14.2 us (3%)
    pallas_call x1, Pallas kernels, experts_main(): pl.pallas_call(functools.partial(experts_kernel, experts=experts), out_sh...  57.5 us
    ppermute x9, waiting for transfers between devices, ring_scatter(): lax.ppermute(parts[shift], 'mp', [(i, (i - shift) % width) for i in range...  52.6 us
    pallas_call x2, Pallas kernels, slab_product(): pl.pallas_call(functools.partial(slab_kernel, experts=experts), out_shape...  33.5 us
    ppermute x9, starting transfers between devices, ring_gather(): lax.ppermute(block, 'mp', [(i, (i + shift) % width) for i in range(width)])  28.6 us
    pallas_call x2, Pallas kernels, experts_before(): pl.pallas_call(functools.partial(before_kernel, count=count, shared=share...  28.2 us
    pallas_call x1, Pallas kernels, experts_out(): pl.pallas_call(functools.partial(branch_kernel, experts=experts), out_sha...  27.2 us
    ppermute x9, waiting for transfers between devices, ring_gather(): lax.ppermute(block, 'mp', [(i, (i + shift) % width) for i in range(width)])  23.9 us
    ppermute x9, starting transfers between devices, ring_scatter(): lax.ppermute(parts[shift], 'mp', [(i, (i - shift) % width) for i in range...  23.8 us
  transfers between devices with their start and end apart: 28, of which 11 were waited for; matrix products, arithmetic and copies ran while one was open for 13% of the time, Pallas kernels for 34%

profile of v2, /device:TPU:0, one launch (start us, length us, event | category | flops | bytes accessed | tf_op | source)
XLA Modules:
  0.0 516.7 jit_solution(12858550795504862007)
XLA Ops:
  18.5 9.2 %all-gather = bf16[8,3,768]{2,1,0:T(4,128)(2,1)S(1)} all-gather(bf16[1,3,768]{2,1,0:T(4,128)(2,1)S(1)} %bitcast.109), channel_id=1, replica_groups=mesh['dp'=8,'mp'=4] {'dp'}, dimensions={0}, use_global_device_ids=true | all-gather | bytes 41472 | tf_op jit(solution)/shard_map/all_gather | solution.py:942
  35.9 23.3 %collective-permute-done.1.refs_7_ = bf16[416,768]{1,0:T(8,128)(2,1)} collective-permute-done((bf16[416,768]{1,0:T(8,128)(2,1)}, bf16[416,768]{1,0:T(8,128)(2,1)}, u32[]{:S(2)}, u32[]{:S(2)}) %collective-permute-start.1) | collective-permute-done | bytes 639008 | tf_op jit(solution)/shard_map/ppermute | solution.py:46
  59.3 14.7 %collective-permute-start.3 = (bf16[384,768]{1,0:T(8,128)(2,1)S(1)}, bf16[384,768]{1,0:T(8,128)(2,1)}, u32[]{:S(2)}, u32[]{:S(2)}) collective-permute-start(bf16[384,768]{1,0:T(8,128)(2,1)S(1)} %copy-done.5), channel_id=1, source_target_pairs={{0,1},{1,2},{2,3},{3,0},{4,5},{5,6},{6,7},{7,4},{8,9},{9,10},{10,1... | collective-permute-start | bytes 1769480 | tf_op jit(solution)/shard_map/ppermute | solution.py:46
  75.4 11.9 %all_gather.13.refs_4_ = bf16[768,576]{1,0:T(8,128)(2,1)} all-gather(bf16[96,576]{1,0:T(8,128)(2,1)S(1)} %convert_element_type.122), channel_id=1, replica_groups=mesh['dp'=8,'mp'=4] {'dp'}, dimensions={0}, use_global_device_ids=true | all-gather | bytes 995328 | tf_op jit(solution)/shard_map/all_gather | solution.py:951
  92.5 10.2 %norm_one.1 = (bf16[1536,768]{1,0:T(8,128)(2,1)}, bf16[1536,768]{1,0:T(8,128)(2,1)}, bf16[1536,1152]{1,0:T(8,128)(2,1)}, bf16[768,1152]{1,0:T(8,128)(2,1)}) custom-call(s32[1]{0:T(128)} %bitcast.refs_0_.rank_ref, s32[1536,1]{1,0:T(8,128)} %broadcast_in_dim.83.refs_1_, f32[3,4608]{1,0:T(4,128)} %reshape.220.refs_2_.table_ref, ...), custom_call_target="tpu_custom_call" | custom-call | flops 1000000 | bytes 100000 | tf_op jit(solution)/shard_map/norm_one/pallas_call | solution.py:271
  115.7 17.4 %attend.1 = (bf16[192,1536]{1,0:T(8,128)(2,1)}, f32[3,1,1536]{2,1,0:T(1,128)}) custom-call(s32[6]{0:T(128)} %subtract_minimum_fusion.start_ref, s32[6]{0:T(128)} %copy-done.39, bf16[1536,1152]{1,0:T(8,128)(2,1)} %get-tuple-element.147.qkv_ref), custom_call_target="tpu_custom_call" | custom-call | flops 1000000 | bytes 100000 | tf_op jit(solution)/shard_map/attend/pallas_call | solution.py:123
  143.9 5.1 grad_branch.1.branch_ref.a_shared_ref
  149.1 12.6 %experts_before.2 = (bf16[8,480,768]{2,1,0:T(8,128)(2,1)}, bf16[8,480,128]{2,1,0:T(8,128)(2,1)}, bf16[8,480,768]{2,1,0:T(8,128)(2,1)}) custom-call(s32[8,1,1536]{2,1,0:T(1,128)} %copy.195.place_ref.refs_1_, bf16[1536,128]{1,0:T(8,128)(2,1)} %pad_convert_fusion.named_ref, bf16[1536,768]{1,0:T(8,128)(2,1)} %grad_branch.1.branch_ref.a_shared_ref, ...), custom_call_target="tpu_custom_call" | custom-call | flops 1000000 | bytes 100000 | tf_op jit(solution)/shard_map/experts_before/pallas_call | solution.py:597
  161.7 15.6 %experts_before.3 = (bf16[8,480,768]{2,1,0:T(8,128)(2,1)}, bf16[8,480,128]{2,1,0:T(8,128)(2,1)}, bf16[8,480,768]{2,1,0:T(8,128)(2,1)}, bf16[1536,768]{1,0:T(8,128)(2,1)}) custom-call(s32[8,1,1536]{2,1,0:T(1,128)} %copy.195.place_ref.refs_1_, bf16[1536,128]{1,0:T(8,128)(2,1)} %pad_convert_fusion.named_ref, ...), custom_call_target="tpu_custom_call", output_to_operand_aliasing={{0}: (4, {}), {1}: (5, {}), {2}: (6, {})} | custom-call | flops 1000000 | bytes 100000 | tf_op jit(solution)/shard_map/experts_before/pallas_call | solution.py:597
  178.1 12.4 %norm_two.1 = (bf16[1536,768]{1,0:T(8,128)(2,1)}, f32[384,768]{1,0:T(8,128)}, f32[384,768]{1,0:T(8,128)}, bf16[768,384]{1,0:T(8,128)(2,1)}) custom-call(s32[1]{0:T(128)} %bitcast.refs_0_.rank_ref, s32[1536,1]{1,0:T(8,128)} %broadcast_in_dim.83.refs_1_, f32[3,4608]{1,0:T(4,128)} %reshape.220.refs_2_.table_ref, bf16[1536,768]{1,0:T(8,128)(2,1)} %get-tuple-element.148.refs_3_, ...), custom_call_target="tpu_custom_call" | custom-call | flops 1000000 | bytes 100000 | tf_op jit(solution)/shard_map/norm_two/pallas_call | solution.py:366
  190.6 57.5 %experts_main.1 = (bf16[8,480,768]{2,1,0:T(8,128)(2,1)}, bf16[8,480,768]{2,1,0:T(8,128)(2,1)}, bf16[8,480,768]{2,1,0:T(8,128)(2,1)}, f32[8,480,1]{2,1,0:T(8,128)...) custom-call(s32[1]{0:T(128)} %bitcast.refs_0_.rank_ref, ...), custom_call_target="tpu_custom_call" | custom-call | flops 1000000 | bytes 100000 | tf_op jit(solution)/shard_map/experts_main/pallas_call | solution.py:707
  248.1 11.8 %collective-permute-start.10 = (bf16[384,768]{1,0:T(8,128)(2,1)}, bf16[384,768]{1,0:T(8,128)(2,1)S(1)}, u32[]{:S(2)}, u32[]{:S(2)}) collective-permute-start(bf16[384,768]{1,0:T(8,128)(2,1)} %get-tuple-element.185), channel_id=1, source_target_pairs={{0,1},{1,2},{2,3},{3,0},{4,5},{5,6},{6,7},{7,4},{8,9},{9,10},{10,1... | collective-permute-start | bytes 1769480 | tf_op jit(solution)/shard_map/ppermute | solution.py:64
  260.9 17.1 %grad_out.1 = bf16[9,768,768]{2,1,0:T(8,128)(2,1)} custom-call(bf16[8,480,768]{2,1,0:T(8,128)(2,1)} %get-tuple-element.186.a_ref, bf16[8,480,768]{2,1,0:T(8,128)(2,1)} %get-tuple-element.187.b_ref.act_ref, bf16[1536,768]{1,0:T(8,128)(2,1)} %grad_branch.1.branch_ref.a_shared_ref, bf16[1536,768]{1,0:T(8,128)(2,1)} %get-tuple-element.188.b_shared_ref.shared_ref, ...), custom_call_target="tpu_custom_call" | custom-call | flops 1000000 | bytes 100000 | tf_op jit(solution)/shard_map/grad_out/pallas_call | solution.py:790
  278.0 9.2 %collective-permute-done.9.refs_1_ = bf16[384,768]{1,0:T(8,128)(2,1)S(1)} collective-permute-done((bf16[384,768]{1,0:T(8,128)(2,1)}, bf16[384,768]{1,0:T(8,128)(2,1)S(1)}, u32[]{:S(2)}, u32[]{:S(2)}) %collective-permute-start.9) | collective-permute-done | bytes 589856 | tf_op jit(solution)/shard_map/ppermute | solution.py:64
  289.5 27.2 %experts_out.1 = (bf16[384,768]{1,0:T(8,128)(2,1)}, bf16[384,768]{1,0:T(8,128)(2,1)}, bf16[384,768]{1,0:T(8,128)(2,1)}, bf16[384,768]{1,0:T(8,128)(2,1)}) custom-call(s32[1]{0:T(128)} %bitcast.refs_0_.rank_ref, s32[1536,2]{1,0:T(8,128)} %copy.196.refs_3_.picked_ref, f32[8,480,1]{2,1,0:T(8,128)} %get-tuple-element.193.refs_0_.gate_ref, ...), custom_call_target="tpu_custom_call" | custom-call | flops 1000000 | bytes 100000 | tf_op jit(solution)/shard_map/experts_out/pallas_call | solution.py:831
  317.6 6.7 %back_two.1 = (f32[384,768]{1,0:T(8,128)}, bf16[384,768]{1,0:T(8,128)(2,1)}, bf16[4,192,384]{2,1,0:T(8,128)(2,1)}, f32[3,2304]{1,0:T(4,128)}) custom-call(s32[1]{0:T(128)} %bitcast.refs_0_.rank_ref, s32[384,1]{1,0:T(8,128)} %dynamic_slice.4.segment_ref, f32[3,4608]{1,0:T(4,128)} %reshape.220.refs_2_.table_ref, bf16[384,768]{1,0:T(8,128)(2,1)} %get-tuple-element.183.refs_0_, ...), custom_call_target="tpu_custom_call" | custom-call | flops 1000000 | bytes 100000 | tf_op jit(solution)/shard_map/back_two/pallas_call | solution.py:465
  324.3 3.8 all-to-all-start.2
  328.1 3.8 collective-permute-start.12
  332.0 16.4 %grad_in.1 = bf16[9,768,768]{2,1,0:T(8,128)(2,1)} custom-call(bf16[8,480,768]{2,1,0:T(8,128)(2,1)} %get-tuple-element.206.a_ref, bf16[8,480,768]{2,1,0:T(8,128)(2,1)} %get-tuple-element.207.b_ref, bf16[1536,768]{1,0:T(8,128)(2,1)} %get-tuple-element.178.refs_4_.a_shared_ref, bf16[1536,768]{1,0:T(8,128)(2,1)} %get-tuple-element.208.b_shared_ref), custom_call_target="tpu_custom_call" | custom-call | flops 1000000 | bytes 100000 | tf_op jit(solution)/shard_map/grad_in/pallas_call | solution.py:790
  352.7 14.7 %collective-permute-done.13.refs_2_ = bf16[384,768]{1,0:T(8,128)(2,1)} collective-permute-done((bf16[384,768]{1,0:T(8,128)(2,1)}, bf16[384,768]{1,0:T(8,128)(2,1)}, u32[]{:S(2)}, u32[]{:S(2)}) %collective-permute-start.13) | collective-permute-done | bytes 589856 | tf_op jit(solution)/shard_map/ppermute | solution.py:64
  367.4 4.6 reduce-scatter.3.cloned.1.call-done
  382.5 21.6 %attend_back.1.a_ref = bf16[1536,1152]{1,0:T(8,128)(2,1)} custom-call(s32[6]{0:T(128)} %subtract_minimum_fusion.start_ref, s32[6]{0:T(128)} %copy-done.39, bf16[1536,1152]{1,0:T(8,128)(2,1)} %get-tuple-element.147.qkv_ref, bf16[192,1536]{1,0:T(8,128)(2,1)} %bitcast.99, f32[3,1,1536]{2,1,0:T(1,128)} %get-tuple-element.212.log_ref), custom_call_target="tpu_custom_call" | custom-call | flops 1000000 | bytes 100000 | tf_op jit(solution)/shard_map/attend_back/pallas_call | solution.py:185
  408.8 7.9 %grad_h_one.1 = (bf16[416,768]{1,0:T(8,128)(2,1)}, bf16[416,768]{1,0:T(8,128)(2,1)}, bf16[416,768]{1,0:T(8,128)(2,1)}, bf16[416,768]{1,0:T(8,128)(2,1)}) custom-call(s32[1]{0:T(128)} %bitcast.refs_0_.rank_ref, bf16[1536,1152]{1,0:T(8,128)(2,1)} %attend_back.1.a_ref, bf16[768,1152]{1,0:T(8,128)(2,1)} %get-tuple-element.218.b_ref, ...), custom_call_target="tpu_custom_call" | custom-call | flops 1000000 | bytes 100000 | tf_op jit(solution)/shard_map/grad_h_one/pallas_call | solution.py:410
  420.8 6.1 %convolution_convert_fusion = bf16[768,1152]{1,0:T(8,128)(2,1)} fusion(bf16[1536,768]{1,0:T(8,128)(2,1)} %get-tuple-element.227, bf16[1536,1152]{1,0:T(8,128)(2,1)S(1)} %copy-done.2), kind=kOutput, calls=%fused_computation.5 | convolution fusion | flops 2718793728 | bytes 7667712 | tf_op jit(solution)/shard_map/gd,gc->dc/dot_general | solution.py:1072
  429.7 5.4 %collective-permute-done.16.refs_1_ = bf16[416,768]{1,0:T(8,128)(2,1)} collective-permute-done((bf16[416,768]{1,0:T(8,128)(2,1)}, bf16[416,768]{1,0:T(8,128)(2,1)}, u32[]{:S(2)}, u32[]{:S(2)}) %collective-permute-start.16) | collective-permute-done | bytes 639008 | tf_op jit(solution)/shard_map/ppermute | solution.py:64
  435.1 14.2 %collective-permute-done.17.refs_3_ = bf16[416,768]{1,0:T(8,128)(2,1)} collective-permute-done((bf16[416,768]{1,0:T(8,128)(2,1)}, bf16[416,768]{1,0:T(8,128)(2,1)}, u32[]{:S(2)}, u32[]{:S(2)}) %collective-permute-start.17) | collective-permute-done | bytes 639008 | tf_op jit(solution)/shard_map/ppermute | solution.py:64
  450.7 4.2 all-to-all-start.4
  454.9 7.7 %fusion.26 = (bf16[8,768,96]{1,2,0:T(8,128)(2,1)}, f32[8,768,96]{1,2,0:T(8,128)}, f32[8,768,96]{1,2,0:T(8,128)}, f32[8,768,96]{1,2,0:T(8,128)}) fusion(f32[8,768,96]{1,2,0:T(8,128)} %param.57, f32[9,96,768]{2,1,0:T(8,128)S(1)} %copy-done.3, f32[8,768,96]{1,2,0:T(8,128)} %param.58, f32[8,768,96]{1,2,0:T(8,128)} %param.59), kind=kLoop, calls=%fused_computation.97 | loop fusion | flops 9437184 | bytes 17694720 | tf_op jit(solution)/shard_map/convert_element_type | solution.py:862
  465.2 3.7 outcome.1
  477.3 4.7 back_one.1
  483.9 12.3 %all-to-all-start.5 = ((f32[32,1,624]{2,1,0:T(1,128)}), f32[32,1,624]{2,1,0:T(1,128)S(1)}, u32[]{:S(2)}, u32[]{:S(2)}) async-start(f32[32,1,624]{2,1,0:T(1,128)} %copy.207), calls=%async_computation.7 | async-start | bytes 163840 | tf_op jit(solution)/shard_map/all_to_all | solution.py:1109
  496.2 7.7 %fusion.28 = (bf16[8,96,768]{2,1,0:T(8,128)(2,1)}, f32[8,96,768]{2,1,0:T(8,128)}, f32[8,96,768]{2,1,0:T(8,128)}, f32[8,96,768]{2,1,0:T(8,128)}) fusion(f32[8,96,768]{2,1,0:T(8,128)} %param.54, f32[9,96,768]{2,1,0:T(8,128)S(1)} %convert_element_type.141, f32[8,96,768]{2,1,0:T(8,128)} %param.55, f32[8,96,768]{2,1,0:T(8,128)} %param.56), kind=kLoop, calls=%fused_computation.98 | loop fusion | flops 9437184 | bytes 17694720 | tf_op jit(solution)/shard_map/convert_element_type | solution.py:862
  (241 shorter events, 101.0 us)
Async XLA Ops:
  7.2 95.5 %all-gather.4.cloned.1.call-start = ((), (), s32[]{:S(2)}) async-start(), calls=%async_computation.8 | async-start | bytes 11943936 | tf_op jit(solution)/shard_map/all_gather | solution.py:919
  10.4 25.5 %copy-start.12 = (f32[96,576]{1,0:T(8,128)S(1)}, f32[96,576]{1,0:T(8,128)}, u32[]{:S(2)}) copy-start(f32[96,576]{1,0:T(8,128)} %param.42) | copy-start | bytes 663556
  10.4 48.9 %copy-start.5 = (bf16[384,768]{1,0:T(8,128)(2,1)S(1)}, bf16[384,768]{1,0:T(8,128)(2,1)}, u32[]{:S(2)}) copy-start(bf16[384,768]{1,0:T(8,128)(2,1)} %refs_5_.1) | copy-start | bytes 1769476
  10.4 77.7 %copy-start.10 = (f32[96,768]{1,0:T(8,128)S(1)}, f32[96,768]{1,0:T(8,128)}, u32[]{:S(2)}) copy-start(f32[96,768]{1,0:T(8,128)} %param.48) | copy-start | bytes 884740
  11.5 77.9 %copy-start.4 = (f32[8,96,768]{2,1,0:T(8,128)S(1)}, f32[8,96,768]{2,1,0:T(8,128)}, u32[]{:S(2)}) copy-start(f32[8,96,768]{2,1,0:T(8,128)} %param.54) | copy-start | bytes 7077892
  11.5 24.4 %collective-permute-start = (bf16[416,768]{1,0:T(8,128)(2,1)}, bf16[416,768]{1,0:T(8,128)(2,1)}, u32[]{:S(2)}, u32[]{:S(2)}) collective-permute-start(bf16[416,768]{1,0:T(8,128)(2,1)} %fusion.5.refs_5_), channel_id=1, source_target_pairs={{0,1},{1,2},{2,3},{3,0},{4,5},{5,6},{6,7},{7,4},{8,9},{9,10},{10,1... | collective-permute-start | bytes 1916936 | tf_op jit(solution)/shard_map/ppermute | solution.py:46
  14.6 44.7 %collective-permute-start.1 = (bf16[416,768]{1,0:T(8,128)(2,1)}, bf16[416,768]{1,0:T(8,128)(2,1)}, u32[]{:S(2)}, u32[]{:S(2)}) collective-permute-start(bf16[416,768]{1,0:T(8,128)(2,1)} %fusion.5.refs_5_), channel_id=1, source_target_pairs={{0,2},{1,3},{2,0},{3,1},{4,6},{5,7},{6,4},{7,5},{8,10},{9,11},{10,... | collective-permute-start | bytes 1916936 | tf_op jit(solution)/shard_map/ppermute | solution.py:46
  17.1 42.1 %collective-permute-start.2 = (bf16[416,768]{1,0:T(8,128)(2,1)}, bf16[416,768]{1,0:T(8,128)(2,1)}, u32[]{:S(2)}, u32[]{:S(2)}) collective-permute-start(bf16[416,768]{1,0:T(8,128)(2,1)} %fusion.5.refs_5_), channel_id=1, source_target_pairs={{0,3},{1,0},{2,1},{3,2},{4,7},{5,4},{6,5},{7,6},{8,11},{9,8},{10,9... | collective-permute-start | bytes 1916936 | tf_op jit(solution)/shard_map/ppermute | solution.py:46
  32.6 58.1 %all-to-all-start = ((f32[32,1,624]{2,1,0:T(1,128)}), f32[32,1,624]{2,1,0:T(1,128)}, u32[]{:S(2)}, u32[]{:S(2)}) async-start(f32[32,1,624]{2,1,0:T(1,128)} %all_to_all.28), calls=%async_computation | async-start | bytes 163840 | tf_op jit(solution)/shard_map/all_to_all | solution.py:950
  35.9 154.7 %all-gather.6.cloned.1.call-start = ((), (), s32[]{:S(2)}) async-start(), calls=%async_computation.9 | async-start | bytes 11943936 | tf_op jit(solution)/shard_map/all_gather | solution.py:985
  59.3 43.4 %collective-permute-start.3 = (bf16[384,768]{1,0:T(8,128)(2,1)S(1)}, bf16[384,768]{1,0:T(8,128)(2,1)}, u32[]{:S(2)}, u32[]{:S(2)}) collective-permute-start(bf16[384,768]{1,0:T(8,128)(2,1)S(1)} %copy-done.5), channel_id=1, source_target_pairs={{0,1},{1,2},{2,3},{3,0},{4,5},{5,6},{6,7},{7,4},{8,9},{9,10},{10,1... | collective-permute-start | bytes 1769480 | tf_op jit(solution)/shard_map/ppermute | solution.py:46
  74.0 28.7 %collective-permute-start.4 = (bf16[384,768]{1,0:T(8,128)(2,1)S(1)}, bf16[384,768]{1,0:T(8,128)(2,1)}, u32[]{:S(2)}, u32[]{:S(2)}) collective-permute-start(bf16[384,768]{1,0:T(8,128)(2,1)S(1)} %copy-done.5), channel_id=1, source_target_pairs={{0,3},{1,0},{2,1},{3,2},{4,7},{5,4},{6,5},{7,6},{8,11},{9,8},{10,9... | collective-permute-start | bytes 1769480 | tf_op jit(solution)/shard_map/ppermute | solution.py:46
  104.5 29.1 %collective-permute-start.5 = (bf16[384,768]{1,0:T(8,128)(2,1)S(1)}, bf16[384,768]{1,0:T(8,128)(2,1)S(1)}, u32[]{:S(2)}, u32[]{:S(2)}) collective-permute-start(bf16[384,768]{1,0:T(8,128)(2,1)S(1)} %copy-done.5), channel_id=1, source_target_pairs={{0,2},{1,3},{2,0},{3,1},{4,6},{5,7},{6,4},{7,5},{8,10},{9,11},{10,... | collective-permute-start | bytes 1769480 | tf_op jit(solution)/shard_map/ppermute | solution.py:46
  109.9 32.6 %all-to-all-start.1 = ((bf16[8,96,768]{2,1,0:T(8,128)(2,1)}), bf16[8,96,768]{2,1,0:T(8,128)(2,1)S(1)}, u32[]{:S(2)}, u32[]{:S(2)}) async-start(bf16[8,96,768]{2,1,0:T(8,128)(2,1)} %broadcast_in_dim.81), calls=%async_computation.1 | async-start | bytes 2359296 | tf_op jit(solution)/shard_map/all_to_all | solution.py:940
  113.4 258.5 %reduce-scatter.3.cloned.1.call-start = ((), (), s32[]{:S(2)}) async-start(), calls=%async_computation.10 | async-start | bytes 11943936 | tf_op jit(solution)/shard_map/reduce_scatter | solution.py:1038
  133.7 43.6 %collective-permute-start.6 = (bf16[192,1536]{1,0:T(8,128)(2,1)}, bf16[192,1536]{1,0:T(8,128)(2,1)S(1)}, u32[]{:S(2)}, u32[]{:S(2)}) collective-permute-start(bf16[192,1536]{1,0:T(8,128)(2,1)} %get-tuple-element.174.refs_5_), channel_id=1, source_target_pairs={{0,1},{1,2},{2,3},{3,0},{4,5},{5,6},{6,7},{7,4},{8,9},{9,10},{10,1... | collective-permute-start | bytes 1769480 | tf_op jit(solution)/shard_map/ppermute | solution.py:46
  135.2 42.2 %collective-permute-start.7 = (bf16[192,1536]{1,0:T(8,128)(2,1)}, bf16[192,1536]{1,0:T(8,128)(2,1)}, u32[]{:S(2)}, u32[]{:S(2)}) collective-permute-start(bf16[192,1536]{1,0:T(8,128)(2,1)} %get-tuple-element.174.refs_5_), channel_id=1, source_target_pairs={{0,2},{1,3},{2,0},{3,1},{4,6},{5,7},{6,4},{7,5},{8,10},{9,11},{10,... | collective-permute-start | bytes 1769480 | tf_op jit(solution)/shard_map/ppermute | solution.py:46
  136.3 41.1 %collective-permute-start.8 = (bf16[192,1536]{1,0:T(8,128)(2,1)}, bf16[192,1536]{1,0:T(8,128)(2,1)}, u32[]{:S(2)}, u32[]{:S(2)}) collective-permute-start(bf16[192,1536]{1,0:T(8,128)(2,1)} %get-tuple-element.174.refs_5_), channel_id=1, source_target_pairs={{0,3},{1,0},{2,1},{3,2},{4,7},{5,4},{6,5},{7,6},{8,11},{9,8},{10,9... | collective-permute-start | bytes 1769480 | tf_op jit(solution)/shard_map/ppermute | solution.py:46
  248.1 29.9 %collective-permute-start.10 = (bf16[384,768]{1,0:T(8,128)(2,1)}, bf16[384,768]{1,0:T(8,128)(2,1)S(1)}, u32[]{:S(2)}, u32[]{:S(2)}) collective-permute-start(bf16[384,768]{1,0:T(8,128)(2,1)} %get-tuple-element.185), channel_id=1, source_target_pairs={{0,1},{1,2},{2,3},{3,0},{4,5},{5,6},{6,7},{7,4},{8,9},{9,10},{10,1... | collective-permute-start | bytes 1769480 | tf_op jit(solution)/shard_map/ppermute | solution.py:64
  259.9 27.3 %collective-permute-start.9 = (bf16[384,768]{1,0:T(8,128)(2,1)}, bf16[384,768]{1,0:T(8,128)(2,1)S(1)}, u32[]{:S(2)}, u32[]{:S(2)}) collective-permute-start(bf16[384,768]{1,0:T(8,128)(2,1)} %get-tuple-element.184), channel_id=1, source_target_pairs={{0,3},{1,0},{2,1},{3,2},{4,7},{5,4},{6,5},{7,6},{8,11},{9,8},{10,9... | collective-permute-start | bytes 1769480 | tf_op jit(solution)/shard_map/ppermute | solution.py:64
  288.0 28.8 %collective-permute-start.11 = (bf16[384,768]{1,0:T(8,128)(2,1)S(1)}, bf16[384,768]{1,0:T(8,128)(2,1)S(1)}, u32[]{:S(2)}, u32[]{:S(2)}) collective-permute-start(bf16[384,768]{1,0:T(8,128)(2,1)S(1)} %copy-done.42), channel_id=1, source_target_pairs={{0,2},{1,3},{2,0},{3,1},{4,6},{5,7},{6,4},{7,5},{8,10},{9,11},{10,... | collective-permute-start | bytes 1769480 | tf_op jit(solution)/shard_map/ppermute | solution.py:64
  324.3 43.1 %all-to-all-start.2 = ((bf16[4,192,384]{2,1,0:T(8,128)(2,1)}), bf16[4,192,384]{2,1,0:T(8,128)(2,1)S(1)}, u32[]{:S(2)}, u32[]{:S(2)}) async-start(bf16[4,192,384]{2,1,0:T(8,128)(2,1)} %get-tuple-element.202), calls=%async_computation.2 | async-start | bytes 1179648 | tf_op jit(solution)/shard_map/all_to_all | solution.py:1042
  328.1 146.5 %reduce-scatter.5.cloned.1.call-start = ((), (), s32[]{:S(2)}) async-start(), calls=%async_computation.11 | async-start | bytes 11943936 | tf_op jit(solution)/shard_map/reduce_scatter | solution.py:1053
  328.1 24.6 %collective-permute-start.12 = (bf16[384,768]{1,0:T(8,128)(2,1)}, bf16[384,768]{1,0:T(8,128)(2,1)S(1)}, u32[]{:S(2)}, u32[]{:S(2)}) collective-permute-start(bf16[384,768]{1,0:T(8,128)(2,1)} %get-tuple-element.209), channel_id=1, source_target_pairs={{0,3},{1,0},{2,1},{3,2},{4,7},{5,4},{6,5},{7,6},{8,11},{9,8},{10,9... | collective-permute-start | bytes 1769480 | tf_op jit(solution)/shard_map/ppermute | solution.py:64
  332.0 35.4 %collective-permute-start.13 = (bf16[384,768]{1,0:T(8,128)(2,1)}, bf16[384,768]{1,0:T(8,128)(2,1)}, u32[]{:S(2)}, u32[]{:S(2)}) collective-permute-start(bf16[384,768]{1,0:T(8,128)(2,1)} %get-tuple-element.210), channel_id=1, source_target_pairs={{0,1},{1,2},{2,3},{3,0},{4,5},{5,6},{6,7},{7,4},{8,9},{9,10},{10,1... | collective-permute-start | bytes 1769480 | tf_op jit(solution)/shard_map/ppermute | solution.py:64
  374.7 29.3 %all-to-all-start.3 = ((bf16[8,96,768]{2,1,0:T(8,128)(2,1)}), bf16[8,96,768]{2,1,0:T(8,128)(2,1)S(1)}, u32[]{:S(2)}, u32[]{:S(2)}) async-start(bf16[8,96,768]{2,1,0:T(8,128)(2,1)} %bitcast.21), calls=%async_computation.4 | async-start | bytes 2359296 | tf_op jit(solution)/shard_map/all_to_all | solution.py:933
  378.3 29.4 %collective-permute-start.14 = (bf16[384,768]{1,0:T(8,128)(2,1)}, bf16[384,768]{1,0:T(8,128)(2,1)S(1)}, u32[]{:S(2)}, u32[]{:S(2)}) collective-permute-start(bf16[384,768]{1,0:T(8,128)(2,1)} %get-tuple-element.216), channel_id=1, source_target_pairs={{0,2},{1,3},{2,0},{3,1},{4,6},{5,7},{6,4},{7,5},{8,10},{9,11},{10,... | collective-permute-start | bytes 1769480 | tf_op jit(solution)/shard_map/ppermute | solution.py:64
  416.7 18.4 %collective-permute-start.16 = (bf16[416,768]{1,0:T(8,128)(2,1)}, bf16[416,768]{1,0:T(8,128)(2,1)}, u32[]{:S(2)}, u32[]{:S(2)}) collective-permute-start(bf16[416,768]{1,0:T(8,128)(2,1)} %get-tuple-element.225), channel_id=1, source_target_pairs={{0,3},{1,0},{2,1},{3,2},{4,7},{5,4},{6,5},{7,6},{8,11},{9,8},{10,9... | collective-permute-start | bytes 1916936 | tf_op jit(solution)/shard_map/ppermute | solution.py:64
  420.0 29.3 %collective-permute-start.17 = (bf16[416,768]{1,0:T(8,128)(2,1)}, bf16[416,768]{1,0:T(8,128)(2,1)}, u32[]{:S(2)}, u32[]{:S(2)}) collective-permute-start(bf16[416,768]{1,0:T(8,128)(2,1)} %get-tuple-element.226), channel_id=1, source_target_pairs={{0,1},{1,2},{2,3},{3,0},{4,5},{5,6},{6,7},{7,4},{8,9},{9,10},{10,1... | collective-permute-start | bytes 1916936 | tf_op jit(solution)/shard_map/ppermute | solution.py:64
  420.3 54.4 %collective-permute-start.15 = (bf16[416,768]{1,0:T(8,128)(2,1)}, bf16[416,768]{1,0:T(8,128)(2,1)}, u32[]{:S(2)}, u32[]{:S(2)}) collective-permute-start(bf16[416,768]{1,0:T(8,128)(2,1)} %get-tuple-element.220), channel_id=1, source_target_pairs={{0,2},{1,3},{2,0},{3,1},{4,6},{5,7},{6,4},{7,5},{8,10},{9,11},{10,... | collective-permute-start | bytes 1916936 | tf_op jit(solution)/shard_map/ppermute | solution.py:64
  450.7 19.0 %all-to-all-start.4 = ((bf16[8,96,576]{2,1,0:T(8,128)(2,1)}), bf16[8,96,576]{2,1,0:T(8,128)(2,1)}, u32[]{:S(2)}, u32[]{:S(2)}) async-start(bf16[8,96,576]{2,1,0:T(8,128)(2,1)} %bitcast.97), calls=%async_computation.5 | async-start | bytes 1966080 | tf_op jit(solution)/shard_map/all_to_all | solution.py:933
  483.9 23.4 %all-to-all-start.5 = ((f32[32,1,624]{2,1,0:T(1,128)}), f32[32,1,624]{2,1,0:T(1,128)S(1)}, u32[]{:S(2)}, u32[]{:S(2)}) async-start(f32[32,1,624]{2,1,0:T(1,128)} %copy.207), calls=%async_computation.7 | async-start | bytes 163840 | tf_op jit(solution)/shard_map/all_to_all | solution.py:1109
  (42 other events, 287.6 us)
Sparse Core Ops, SparseCore 0:
  10.5 67.3 all-gather.3
  102.9 75.1 all-gather.5
  287.3 84.5 reduce-scatter.2
  375.3 82.2 reduce-scatter.4
